TPU v7x, 32 devices: a whole 2x2x4 slice. The times are simulated.
32 devices in a mesh: batch: 4 (over z), tm: 8 (over y, x, core).
Axes of the slice: x: 2, y: 2, z: 4, core: 2. Of those that a mesh axis runs over, the one named last changes fastest.
Arguments:
- frames: bfloat16 [16, 512, 512], P('batch', 'tm'), may hold values from -6 to 6
- noise: float32 [16, 32, 512], P('batch', None, 'tm'), may hold values from -4 to 7.5
- frame_lengths: int32 [16], P('batch'), may hold values from 64 to 512, as said below
- labels: int32 [16, 32], P('batch'), may hold values from 1 to 999
- label_lengths: int32 [16], P('batch'), may hold values from 16 to 32, as said below
- w_in: bfloat16 [512, 4096], P(None, ('batch', 'tm')), may hold values from -0.25 to 0.25
- w_rec: bfloat16 [1024, 4096], P(None, ('batch', 'tm')), may hold values from -0.1875 to 0.1875
- ln_gain: float32 [4096], replicated, may hold values from 0.5 to 1.5
- ln_shift: float32 [4096], replicated, may hold values from -1.5 to 1.5
- init_state: float32 [2, 1024], replicated, may hold values from -3 to 3
- dec_table: bfloat16 [1000, 4096], P(None, ('batch', 'tm')), may hold values from -3 to 3
- dec_rec: bfloat16 [1024, 4096], P(None, ('batch', 'tm')), may hold values from -0.1875 to 0.1875
- att_query: bfloat16 [1024, 2048], P(None, ('batch', 'tm')), may hold values from -0.1875 to 0.1875
- att_key: bfloat16 [1024, 2048], P(None, ('batch', 'tm')), may hold values from -0.1875 to 0.1875
- att_bias: float32 [2, 1024], replicated, may hold values from -1.5 to 1.5
- att_vec: float32 [2, 1024], replicated, may hold values from -0.5 to 0.5
- monotonic: float32 [2], replicated, may hold values from -7.5 to 2, as said below
- proj_w: bfloat16 [2048, 1024], P(None, ('batch', 'tm')), may hold values from -0.125 to 0.125
- proj_b: float32 [1024], replicated, may hold values from -1.5 to 1.5
- out_w: bfloat16 [1024, 1000], P(('batch', 'tm')), may hold values from -0.5 to 0.5
- out_b: float32 [1000], replicated, may hold values from -2.5 to 2.5
Outputs:
- loss: float32 [], replicated
- frames_grad: float32 [16, 512, 512], P('batch', 'tm')
- w_in_grad: float32 [512, 4096], P(None, ('batch', 'tm'))
- w_rec_grad: float32 [1024, 4096], P(None, ('batch', 'tm'))
- ln_gain_grad: float32 [4096], replicated
- ln_shift_grad: float32 [4096], replicated
- init_state_grad: float32 [2, 1024], replicated
- dec_table_grad: float32 [1000, 4096], P(None, ('batch', 'tm'))
- dec_rec_grad: float32 [1024, 4096], P(None, ('batch', 'tm'))
- att_query_grad: float32 [1024, 2048], P(None, ('batch', 'tm'))
- att_key_grad: float32 [1024, 2048], P(None, ('batch', 'tm'))
- att_bias_grad: float32 [2, 1024], replicated
- att_vec_grad: float32 [2, 1024], replicated
- monotonic_grad: float32 [2], replicated
- proj_w_grad: float32 [2048, 1024], P(None, ('batch', 'tm'))
- proj_b_grad: float32 [1024], replicated
- out_w_grad: float32 [1024, 1000], P(('batch', 'tm'))
- out_b_grad: float32 [1000], replicated
Inputs may be any that keep to these rules, and one draw needn't show every extreme that they name: `frame_lengths`: in every aligned block of 4 utterances one has all 512 frames. `label_lengths`: in every aligned block of 4 utterances one has all 32 labels. `labels`: label 0 is the start symbol and is never a target. `monotonic`: the first entry is g, the second r.
All inputs are finite; a program needn't handle non-finite values.
Results may differ from a plain program's by a relative error of at most 0.014.
Values may be sent and summed in bfloat16 or wider, within the bound.
No kernel may reach another device: no remote copies, remote signals or barrier semaphores. Data moves between devices by JAX's collectives and lax.ppermute only.
A program may use at most 256 MiB of HBM per device.

v0:
```python
import jax
import jax.numpy as jnp
from jax import lax
from jax.sharding import PartitionSpec as P

BLOCK = 16


norm_eps = 1e-05
highest = lax.Precision.HIGHEST


def carried_in(value, axis, join, neutral, backward):
    count, mine = (lax.axis_size(axis), lax.axis_index(axis))
    pieces = lax.all_gather(value, axis)
    if backward:
        pieces = pieces[::-1]
        mine = count - 1 - mine
    running = jnp.full_like(value, 0) + jnp.asarray(neutral, value.dtype)

    def lap(position, running):
        longer = join(running, pieces[position])
        return jnp.where(position < mine, longer, running)

    return lax.fori_loop(0, count - 1, lap, running)


def for_sending(value):

    def short(part):
        return part.astype(jnp.bfloat16) if part.dtype == jnp.float32 else part

    return jax.tree.map(short, value)


def with_halo(block, sides, width):
    for axis, dim in sides:
        count = lax.axis_size(axis)
        forward = [(i, i + 1) for i in range(count - 1)]
        backward = [(target, source) for source, target in forward]
        low = lax.ppermute(
            lax.slice_in_dim(block, block.shape[dim] - width, None, axis=dim), axis, forward
        )
        high = lax.ppermute(lax.slice_in_dim(block, 0, width, axis=dim), axis, backward)
        block = jnp.concatenate([low, block, high], axis=dim)
    return block


def plain_cell(gate_vals, cell_state):
    in_gate, forget, candidate, out_gate = jnp.split(gate_vals, 4, axis=-1)
    new_cell = jax.nn.sigmoid(forget) * cell_state + jax.nn.sigmoid(in_gate) * jnp.tanh(candidate)
    return (jax.nn.sigmoid(out_gate) * jnp.tanh(new_cell), new_cell)


def norm_cell(preact, cell_state, gain, shift):
    row_mean = jnp.mean(preact, axis=-1, keepdims=True)
    centred = preact - row_mean
    row_var = jnp.mean(centred * centred, axis=-1, keepdims=True)
    gate_vals = centred * lax.rsqrt(row_var + norm_eps) * gain + shift
    return plain_cell(gate_vals, cell_state)


def energy_terms(queries, key_proj, att_bias, att_vec, monotonic):
    width = queries.shape[-1] // 2
    mono_act = jnp.tanh(queries[:, None, :width] + key_proj[None, :, :width] + att_bias[0])
    span_act = jnp.tanh(queries[:, None, width:] + key_proj[None, :, width:] + att_bias[1])
    vec_scale = monotonic[0] * lax.rsqrt(jnp.sum(att_vec[0] * att_vec[0]) + 1e-06)
    mono_energy = jnp.sum(mono_act * att_vec[0], axis=-1) * vec_scale + monotonic[1]
    span_energy = jnp.sum(span_act * att_vec[1], axis=-1)
    return (mono_energy, span_energy)


def forward_dot(left, right):
    return jnp.dot(left, right, preferred_element_type=jnp.float32)


def dot_last(left, right):
    return lax.dot_general(
        left, right, (((left.ndim - 1,), (1,)), ((), ())), preferred_element_type=jnp.float32
    )


def dot_first(left, right):
    return lax.dot_general(
        left, right, (((0,), (0,)), ((), ())), preferred_element_type=jnp.float32
    )


def head_rows(states_rows, context_rows, label_ids, label_mask, proj_w, proj_b, out_w, out_b):
    hidden_size = states_rows.shape[-1]
    vocab_size = out_b.shape[0]
    joined = jnp.concatenate([states_rows, context_rows], axis=-1)
    proj_out = jnp.tanh(forward_dot(joined, proj_w) + proj_b)
    proj_low = proj_out.astype(jnp.bfloat16)
    logits = forward_dot(proj_low, out_w) + out_b
    log_norm = jax.nn.logsumexp(logits, axis=-1)
    target = (label_ids[:, None] == jnp.arange(vocab_size)[None, :]).astype(jnp.float32)
    picked = jnp.sum(logits * target, axis=-1)
    total_loss = jnp.sum((log_norm - picked) * label_mask)
    logit_grad = (jnp.exp(logits - log_norm[:, None]) - target) * label_mask[:, None]
    logit_low = logit_grad.astype(jnp.bfloat16)
    out_w_grad = dot_first(proj_low, logit_low)
    proj_grad = dot_last(logit_low, out_w) * (1.0 - proj_out * proj_out)
    proj_low_grad = proj_grad.astype(jnp.bfloat16)
    proj_w_grad = dot_first(joined, proj_low_grad)
    joined_grad = dot_last(proj_low_grad, proj_w)
    return (
        total_loss,
        jnp.sum(logit_grad, axis=0),
        out_w_grad,
        jnp.sum(proj_grad, axis=0),
        proj_w_grad,
        joined_grad[:, :hidden_size],
        joined_grad[:, hidden_size:].astype(jnp.bfloat16),
    )


def local(
    frames,
    noise,
    frame_lengths,
    labels,
    label_lengths,
    w_in,
    w_rec,
    ln_gain,
    ln_shift,
    init_state,
    dec_table,
    dec_rec,
    att_query,
    att_key,
    att_bias,
    att_vec,
    monotonic,
    proj_w,
    proj_b,
    out_w,
    out_b,
):
    full_in, full_rec, full_table, full_dec, full_query, full_key, full_proj, full_out = (
        lax.all_gather(w_in, ("batch", "tm"), axis=1, tiled=True),
        lax.all_gather(w_rec, ("batch", "tm"), axis=1, tiled=True),
        lax.all_gather(dec_table, ("batch", "tm"), axis=1, tiled=True),
        lax.all_gather(dec_rec, ("batch", "tm"), axis=1, tiled=True),
        lax.all_gather(att_query, ("batch", "tm"), axis=1, tiled=True),
        lax.all_gather(att_key, ("batch", "tm"), axis=1, tiled=True),
        lax.all_gather(proj_w, ("batch", "tm"), axis=1, tiled=True),
        lax.all_gather(out_w, ("batch", "tm"), axis=0, tiled=True),
    )
    utterances, frame_count, feat_size = frames.shape
    label_steps = labels.shape[1]
    hidden_size = full_rec.shape[0]
    gate_width = 4 * hidden_size
    vocab_size = out_b.shape[0]
    time_index = lax.axis_index("tm")
    first_time = (time_index == 0).astype(jnp.float32)
    block_count = frame_count // BLOCK
    enc_rows = utterances * block_count
    step_in = forward_dot(frames.reshape(-1, feat_size), full_in)
    step_in = (
        step_in.reshape(utterances, block_count, BLOCK, gate_width)
        .transpose(2, 0, 1, 3)
        .reshape(BLOCK, enc_rows, gate_width)
    )
    start_hidden = jnp.broadcast_to(init_state[0].astype(jnp.bfloat16), (enc_rows, hidden_size))
    start_cell = jnp.broadcast_to(init_state[1], (enc_rows, hidden_size))

    def enc_step(state_carry, step_input):
        prev_hidden, prev_cell = state_carry
        preact = step_input + forward_dot(prev_hidden, full_rec)
        new_hidden, new_cell = norm_cell(preact, prev_cell, ln_gain, ln_shift)
        new_hidden = new_hidden.astype(jnp.bfloat16)
        return ((new_hidden, new_cell), (preact, prev_cell, prev_hidden, new_hidden))

    enc_final, (enc_pre, enc_cprev, enc_hprev, enc_out) = lax.scan(
        enc_step, (start_hidden, start_cell), step_in
    )
    memory = (
        enc_out.reshape(BLOCK, utterances, block_count, hidden_size)
        .transpose(1, 2, 0, 3)
        .reshape(utterances, frame_count, hidden_size)
    )
    key_proj = forward_dot(memory.reshape(-1, hidden_size), full_key).reshape(
        utterances, frame_count, -1
    )
    prev_ids = jnp.concatenate([jnp.zeros((utterances, 1), jnp.int32), labels[:, :-1]], axis=1)
    prev_onehot = prev_ids.reshape(-1)[:, None] == jnp.arange(vocab_size)[None, :]
    table_rows = forward_dot(prev_onehot.astype(jnp.bfloat16), full_table).reshape(
        utterances, label_steps, gate_width
    )
    zero_state = jnp.zeros((utterances, hidden_size), jnp.float32)

    def dec_step(state_carry, table_row):
        prev_state, prev_cell = state_carry
        preact = table_row + forward_dot(prev_state, full_dec)
        new_state, new_cell = plain_cell(preact, prev_cell)
        new_state = new_state.astype(jnp.bfloat16)
        return ((new_state, new_cell), (preact, prev_cell, prev_state, new_state))

    dec_final, (dec_pre, dec_cprev, dec_sprev, dec_out) = lax.scan(
        dec_step, (zero_state.astype(jnp.bfloat16), zero_state), jnp.swapaxes(table_rows, 0, 1)
    )
    states = jnp.swapaxes(dec_out, 0, 1)
    states_flat = states.reshape(-1, hidden_size)
    queries = forward_dot(states_flat, full_query).reshape(utterances, label_steps, -1)

    def energy_forward(packed):
        return energy_terms(packed[0], packed[1], att_bias, att_vec, monotonic)

    mono_energy, span_energy = lax.map(energy_forward, (queries, key_proj))
    energy = mono_energy + noise
    positions = time_index * frame_count + jnp.arange(frame_count)
    frame_mask = (positions[None, :] < frame_lengths[:, None]).astype(jnp.float32)[:, None, :]
    sig_energy = jax.nn.sigmoid(energy)
    stop_prob = sig_energy * frame_mask
    survive = jnp.cumprod(1.0 - stop_prob, axis=-1)
    carried = carried_in(
        survive[..., -1],
        "tm",
        lambda earlier, later: earlier * later,
        jnp.ones_like(survive[..., -1]),
        False,
    )
    before = carried[..., None] * jnp.concatenate(
        [jnp.ones_like(survive[..., :1]), survive[..., :-1]], axis=-1
    )
    alignment = stop_prob * before
    rim_values = with_halo(for_sending(jnp.stack([span_energy, alignment])), (("tm", 3),), 1)
    span_ext = rim_values[0]
    align_ext = rim_values[1]
    ext_positions = time_index * frame_count + jnp.arange(frame_count + 1)
    share_ext = jnp.where(
        ext_positions == 0, 1.0, jax.nn.sigmoid(span_ext[..., 1:] - span_ext[..., :-1])
    )
    self_share = share_ext[..., :-1]
    next_share = share_ext[..., 1:]
    next_align = align_ext[..., 2:]
    span_weight = alignment * self_share + next_align * (1.0 - next_share)
    weight_low = span_weight.astype(jnp.bfloat16)
    context_part = jnp.einsum(
        "buf,bfh->buh", weight_low, memory, preferred_element_type=jnp.float32
    )
    head_count = utterances * label_steps
    label_flat = labels.reshape(-1)
    label_mask = (
        (jnp.arange(label_steps)[None, :] < label_lengths[:, None]).astype(jnp.float32).reshape(-1)
    )
    context_all = lax.psum(context_part.astype(jnp.bfloat16), "tm").astype(jnp.float32)
    results = head_rows(
        states_flat,
        context_all.reshape(head_count, hidden_size).astype(jnp.bfloat16),
        label_flat,
        label_mask,
        full_proj,
        proj_b,
        full_out,
        out_b,
    )
    total_loss, grad_out_b, grad_out_w, grad_proj_b, grad_proj_w = tuple(
        (member * first_time for member in results[:5])
    )
    state_head = results[5]
    context_grad = results[6]
    context_grid = context_grad.reshape(utterances, label_steps, hidden_size)
    weight_grad = jnp.einsum(
        "buh,bfh->buf", context_grid, memory, preferred_element_type=jnp.float32
    )
    memory_grad = jnp.einsum(
        "buf,buh->bfh", weight_low, context_grid, preferred_element_type=jnp.float32
    )
    grad_ext = with_halo(weight_grad.astype(jnp.bfloat16), (("tm", 2),), 1).astype(
        weight_grad.dtype
    )
    prev_grad = grad_ext[..., :-2]
    next_grad = grad_ext[..., 2:]
    align_grad = weight_grad * self_share + prev_grad * (1.0 - self_share)
    here_term = alignment * (weight_grad - prev_grad) * self_share * (1.0 - self_share)
    next_term = next_align * (next_grad - weight_grad) * next_share * (1.0 - next_share)
    span_grad = here_term - next_term
    weighted = align_grad * alignment
    suffix_incl = jnp.flip(jnp.cumsum(jnp.flip(weighted, -1), axis=-1), -1)
    later_sum = carried_in(
        suffix_incl[..., 0],
        "tm",
        lambda earlier, later: earlier + later,
        jnp.zeros_like(suffix_incl[..., 0]),
        True,
    )
    after_sum = suffix_incl - weighted + later_sum[..., None]
    stop_grad = align_grad * before - after_sum / (1.0 - stop_prob)
    energy_grad = stop_grad * sig_energy * (1.0 - sig_energy) * frame_mask

    def energy_backward(packed):
        query_rows, key_rows, mono_cot, span_cot = packed
        outputs, pullback = jax.vjp(
            energy_terms, query_rows, key_rows, att_bias, att_vec, monotonic
        )
        return pullback((mono_cot, span_cot))

    query_part, key_grad, bias_grads, vec_grads, mono_grads = lax.map(
        energy_backward, (queries, key_proj, energy_grad, span_grad)
    )
    back_in, back_rec, back_dec, back_query, back_key = (
        lax.all_gather(w_in, ("batch", "tm"), axis=1, tiled=True),
        lax.all_gather(w_rec, ("batch", "tm"), axis=1, tiled=True),
        lax.all_gather(dec_rec, ("batch", "tm"), axis=1, tiled=True),
        lax.all_gather(att_query, ("batch", "tm"), axis=1, tiled=True),
        lax.all_gather(att_key, ("batch", "tm"), axis=1, tiled=True),
    )
    query_total = lax.psum(query_part.astype(jnp.bfloat16), "tm").astype(jnp.float32)
    query_low = query_total.reshape(head_count, -1).astype(jnp.bfloat16)
    state_grad = state_head + dot_last(query_low, back_query)
    key_low = key_grad.reshape(utterances * frame_count, -1).astype(jnp.bfloat16)
    grad_att_key = dot_first(memory.reshape(-1, hidden_size), key_low)
    memory_grad = memory_grad + dot_last(key_low, back_key).reshape(
        utterances, frame_count, hidden_size
    )
    state_seq = jnp.swapaxes(state_grad.reshape(utterances, label_steps, hidden_size), 0, 1)

    def dec_back(grad_carry, packed):
        rec_grad, cell_grad = grad_carry
        preact, prev_cell, out_grad = packed
        outputs, pullback = jax.vjp(plain_cell, preact, prev_cell)
        pre_grad, prev_cell_grad = pullback((out_grad + rec_grad, cell_grad))
        pre_low = pre_grad.astype(jnp.bfloat16)
        return ((dot_last(pre_low, back_dec), prev_cell_grad), (pre_grad, pre_low))

    dec_start, (dec_pre_grad, dec_pre_low) = lax.scan(
        dec_back, (zero_state, zero_state), (dec_pre, dec_cprev, state_seq), reverse=True
    )
    dec_sprev_flat = dec_sprev.reshape(-1, hidden_size)
    dec_low_flat = dec_pre_low.reshape(-1, gate_width)
    dec_grad_rows = jnp.swapaxes(dec_pre_grad, 0, 1).reshape(-1, gate_width)
    onehot_float = prev_onehot.astype(jnp.float32)
    memory_steps = (
        memory_grad.reshape(utterances, block_count, BLOCK, hidden_size)
        .transpose(2, 0, 1, 3)
        .reshape(BLOCK, enc_rows, hidden_size)
    )
    zero_rows = jnp.zeros((enc_rows, hidden_size), jnp.float32)

    def enc_back(grad_carry, packed):
        rec_grad, cell_grad = grad_carry
        preact, prev_cell, out_grad = packed
        outputs, pullback = jax.vjp(norm_cell, preact, prev_cell, ln_gain, ln_shift)
        pre_grad, prev_cell_grad, gain_grad, shift_grad = pullback((out_grad + rec_grad, cell_grad))
        pre_low = pre_grad.astype(jnp.bfloat16)
        return ((dot_last(pre_low, back_rec), prev_cell_grad), (pre_low, gain_grad, shift_grad))

    (start_grad_hidden, start_grad_cell), (enc_pre_low, gain_grads, shift_grads) = lax.scan(
        enc_back, (zero_rows, zero_rows), (enc_pre, enc_cprev, memory_steps), reverse=True
    )
    grad_w_rec = dot_first(enc_hprev.reshape(-1, hidden_size), enc_pre_low.reshape(-1, gate_width))
    frame_pre = (
        enc_pre_low.reshape(BLOCK, utterances, block_count, gate_width)
        .transpose(1, 2, 0, 3)
        .reshape(-1, gate_width)
    )
    grad_w_in = dot_first(frames.reshape(-1, feat_size), frame_pre)
    frames_grad = dot_last(frame_pre, back_in).reshape(utterances, frame_count, feat_size)
    grad_init = jnp.stack([jnp.sum(start_grad_hidden, axis=0), jnp.sum(start_grad_cell, axis=0)])
    grad_att_query = dot_first(states_flat, query_low) * first_time
    grad_dec_rec = dot_first(dec_sprev_flat, dec_low_flat) * first_time
    grad_table = (
        lax.dot_general(
            onehot_float,
            dec_grad_rows,
            (((0,), (0,)), ((), ())),
            precision=highest,
            preferred_element_type=jnp.float32,
        )
        * first_time
    )
    table_out, dec_rec_out, query_out, key_out, proj_w_out, out_w_out = (
        lax.psum_scatter(grad_table, ("batch", "tm"), scatter_dimension=1, tiled=True),
        lax.psum_scatter(grad_dec_rec, ("batch", "tm"), scatter_dimension=1, tiled=True),
        lax.psum_scatter(grad_att_query, ("batch", "tm"), scatter_dimension=1, tiled=True),
        lax.psum_scatter(grad_att_key, ("batch", "tm"), scatter_dimension=1, tiled=True),
        lax.psum_scatter(grad_proj_w, ("batch", "tm"), scatter_dimension=1, tiled=True),
        lax.psum_scatter(grad_out_w, ("batch", "tm"), scatter_dimension=0, tiled=True),
    )
    w_in_out, w_rec_out = (
        lax.psum_scatter(grad_w_in, ("batch", "tm"), scatter_dimension=1, tiled=True),
        lax.psum_scatter(grad_w_rec, ("batch", "tm"), scatter_dimension=1, tiled=True),
    )
    loss_out, init_out, gain_out, shift_out, bias_out, vec_out, mono_out, proj_b_out, out_b_out = (
        lax.psum(
            (
                total_loss,
                grad_init,
                jnp.sum(gain_grads, axis=0),
                jnp.sum(shift_grads, axis=0),
                jnp.sum(bias_grads, axis=0),
                jnp.sum(vec_grads, axis=0),
                jnp.sum(mono_grads, axis=0),
                grad_proj_b,
                grad_out_b,
            ),
            ("batch", "tm"),
        )
    )
    return (
        loss_out,
        frames_grad,
        w_in_out,
        w_rec_out,
        gain_out,
        shift_out,
        init_out,
        table_out,
        dec_rec_out,
        query_out,
        key_out,
        bias_out,
        vec_out,
        mono_out,
        proj_w_out,
        proj_b_out,
        out_w_out,
        out_b_out,
    )


def solution(mesh):
    return jax.shard_map(
        local,
        mesh=mesh,
        in_specs=(
            P("batch", "tm", None),
            P("batch", None, "tm"),
            P("batch"),
            P("batch", None),
            P("batch"),
            P(None, ("batch", "tm")),
            P(None, ("batch", "tm")),
            P(),
            P(),
            P(),
            P(None, ("batch", "tm")),
            P(None, ("batch", "tm")),
            P(None, ("batch", "tm")),
            P(None, ("batch", "tm")),
            P(),
            P(),
            P(),
            P(None, ("batch", "tm")),
            P(),
            P(("batch", "tm"), None),
            P(),
        ),
        out_specs=(
            P(),
            P("batch", "tm", None),
            P(None, ("batch", "tm")),
            P(None, ("batch", "tm")),
            P(),
            P(),
            P(),
            P(None, ("batch", "tm")),
            P(None, ("batch", "tm")),
            P(None, ("batch", "tm")),
            P(None, ("batch", "tm")),
            P(),
            P(),
            P(),
            P(None, ("batch", "tm")),
            P(),
            P(("batch", "tm"), None),
            P(),
        ),
        check_vma=False,
    )
```

profile of v0, /device:TPU:0, one launch (start us, length us, event | category | flops | bytes accessed | tf_op | source)
XLA Modules:
  0.0 2542.4 jit_solution(5952912651305471431)
XLA Ops:
  18.3 60.7 %all-gather.17.cloned.1.call-done = bf16[512,4096]{1,0:T(8,128)(2,1)} async-done(((bf16[512,128]{1,0:T(8,128)(2,1)}), bf16[512,4096]{1,0:T(8,128)(2,1)}) %all-gather.17.cloned.1.call-update) | async-done | bytes 4194320 | tf_op jit(solution)/shard_map/all_gather | solution.py:142
  84.4 86.7 %all-gather.11.cloned.1.call-done = bf16[1000,4096]{1,0:T(8,128)(2,1)} async-done(((bf16[1000,128]{1,0:T(8,128)(2,1)}), bf16[1000,4096]{1,0:T(8,128)(2,1)}) %all-gather.11.cloned.1.call-update) | async-done | bytes 8192016 | tf_op jit(solution)/shard_map/all_gather | solution.py:144
  177.4 87.1 %all-gather.19.cloned.1.call-done = bf16[1024,4096]{1,0:T(8,128)(2,1)} async-done(((bf16[1024,128]{1,0:T(8,128)(2,1)}), bf16[1024,4096]{1,0:T(8,128)(2,1)}) %all-gather.19.cloned.1.call-update) | async-done | bytes 8388624 | tf_op jit(solution)/shard_map/all_gather | solution.py:143
  264.5 144.6 %while.147 = (s32[]{:T(128)}, bf16[16,1024]{1,0:T(8,128)(2,1)S(1)}, f32[16,1024]{1,0:T(8,128)S(1)}, f32[16,16,4096]{2,1,0:T(8,128)}, f32[16,16,1024]{2,1,0:T(8,1...) while((s32[]{:T(128)}, bf16[16,1024]{1,0:T(8,128)(2,1)S(1)}, ...), condition=%wide.region_5.6_spmd, body=%wide.region_2.5_spmd.sunk | while | flops 135036944 | bytes 11471033 | solution.py:176
  410.4 209.0 %while.150 = (s32[]{:T(128)}, bf16[4,1024]{1,0:T(4,128)(2,1)S(1)}, f32[4,1024]{1,0:T(4,128)S(1)}, f32[32,4,4096]{2,1,0:T(4,128)}, f32[32,4,1024]{2,1,0:T(4,128)}...) while((s32[]{:T(128)}, bf16[4,1024]{1,0:T(4,128)(2,1)S(1)}, ...), condition=%wide.region_1.0_spmd.clone, body=%wide.region_0.1_spmd.clone.sunk | while | flops 33644544 | bytes 8758905 | solution.py:201
  626.8 23.1 while.148
  655.6 8.8 all-gather
  664.5 8.2 while.151
  688.9 50.5 %all-reduce.17.cloned.1.call-done = bf16[128,1024]{1,0:T(8,128)(2,1)} async-done(((bf16[128,1024]{1,0:T(8,128)(2,1)}), bf16[128,1024]{1,0:T(8,128)(2,1)}) %all-reduce.17.cloned.1.call-update) | async-done | bytes 262160 | tf_op jit(solution)/shard_map/psum | solution.py:249
  744.2 54.4 %all-gather.25.cloned.1.call-done = bf16[1024,1000]{1,0:T(8,128)(2,1)} async-done(((bf16[32,1000]{1,0:T(8,128)(2,1)}), bf16[1024,1000]{1,0:T(8,128)(2,1)}) %all-gather.25.cloned.1.call-update) | async-done | bytes 2048016 | tf_op jit(solution)/shard_map/all_gather | solution.py:149
  825.4 10.8 all-gather.1
  836.2 8.2 while.152
  846.2 110.1 %while.149 = (s32[]{:T(128)}, bf16[4,32,2048]{2,1,0:T(8,128)(2,1)}, bf16[4,64,2048]{2,1,0:T(8,128)(2,1)}, f32[4,2,1024]{2,1,0:T(2,128)}, f32[4,2,1024]{2,1,0:T(2...) while((s32[]{:T(128)}, bf16[4,32,2048]{2,1,0:T(8,128)(2,1)}, ...), condition=%wide.region_35.36_spmd, body=%wide.region_23.35_spmd.sunk | while | flops 54537216 | bytes 11728237 | solution.py:301
  962.9 280.1 %while.153 = (s32[]{:T(128)}, f32[16,1024]{1,0:T(8,128)S(1)}, f32[16,1024]{1,0:T(8,128)S(1)}, bf16[16,16,4096]{2,1,0:T(8,128)(2,1)S(1)}, f32[16,4096]{1,0:T(8,12...) while((s32[]{:T(128)}, f32[16,1024]{1,0:T(8,128)S(1)}, ...), condition=%wide.region_43.44_spmd.clone, body=%wide.region_36.43_spmd.clone.sunk | while | flops 137748592 | bytes 13618767 | solution.py:351
  1280.5 343.8 %while.154 = (s32[]{:T(128)}, f32[4,1024]{1,0:T(4,128)S(1)}, f32[4,1024]{1,0:T(4,128)S(1)}, f32[32,4,4096]{2,0,1:T(8,128)}, bf16[32,4,4096]{2,1,0:T(4,128)(2,1)}...) while((s32[]{:T(128)}, f32[4,1024]{1,0:T(4,128)S(1)}, ...), condition=%wide.region_55.56_spmd.clone, body=%wide.region_54.55_spmd.clone.sunk | while | flops 34078724 | bytes 9486495 | solution.py:329
  1624.3 12.0 convolution_multiply_fusion
  1637.4 9.7 convolution_bitcast_fusion
  1648.1 9.4 bitcast_multiply_fusion.6
  1659.7 43.0 %all-reduce.13 = (f32[]{:T(128)}, f32[4096]{0:T(1024)}, f32[4096]{0:T(1024)}, f32[2,1024]{1,0:T(2,128)}, f32[2,1024]{1,0:T(2,128)}, /*index=5*/f32[2,1024]{1,0:T...) all-reduce(f32[]{:T(128)S(6)} %mul.865, ...), channel_id=1, replica_groups=mesh['batch'=4,'tm'=8] {'batch','tm'}, use_global_device_ids=true, to_apply=%region_19.20 | all-reduce | flops 16363 | bytes 130904 | tf_op jit(solution)/shard_map/psum | solution.py:388
  1709.1 125.2 %reduce-scatter.19.cloned.1.call-done = f32[1024,64]{0,1:T(8,128)} async-done(((f32[1024,2048]{0,1:T(8,128)}), f32[1024,64]{0,1:T(8,128)}) %reduce-scatter.19.cloned.1.call-update) | async-done | bytes 262160 | tf_op jit(solution)/shard_map/reduce_scatter | solution.py:379
  1834.3 147.4 %reduce-scatter.17.cloned.1.call-done = f32[1024,64]{0,1:T(8,128)} async-done(((f32[1024,2048]{0,1:T(8,128)}), f32[1024,64]{0,1:T(8,128)}) %reduce-scatter.17.cloned.1.call-update) | async-done | bytes 262160 | tf_op jit(solution)/shard_map/reduce_scatter | solution.py:378
  1981.8 178.8 %reduce-scatter.13.cloned.1.call-done = f32[1000,128]{1,0:T(8,128)} async-done(((f32[1000,4096]{1,0:T(8,128)}), f32[1000,128]{1,0:T(8,128)}) %reduce-scatter.13.cloned.1.call-update) | async-done | bytes 512016 | tf_op jit(solution)/shard_map/reduce_scatter | solution.py:376
  2160.6 187.2 %reduce-scatter.11.cloned.1.call-done = f32[1024,128]{1,0:T(8,128)} async-done(((f32[1024,4096]{1,0:T(8,128)}), f32[1024,128]{1,0:T(8,128)}) %reduce-scatter.11.cloned.1.call-update) | async-done | bytes 524304 | tf_op jit(solution)/shard_map/reduce_scatter | solution.py:385
  2347.8 187.5 %reduce-scatter.15.cloned.1.call-done = f32[1024,128]{1,0:T(8,128)} async-done(((f32[1024,4096]{1,0:T(8,128)}), f32[1024,128]{1,0:T(8,128)}) %reduce-scatter.15.cloned.1.call-update) | async-done | bytes 524304 | tf_op jit(solution)/shard_map/reduce_scatter | solution.py:377
  (1165 shorter events, 1256.0 us)
Async XLA Ops:
  7.2 71.8 %all-gather.17.cloned.1.call-start = ((), (), s32[]{:S(2)}) async-start(), calls=%async_computation.11 | async-start | bytes 4325376 | tf_op jit(solution)/shard_map/all_gather | solution.py:142
  7.9 163.2 %all-gather.11.cloned.1.call-start = ((), (), s32[]{:S(2)}) async-start(), calls=%async_computation.8 | async-start | bytes 8448000 | tf_op jit(solution)/shard_map/all_gather | solution.py:144
  8.7 255.8 %all-gather.19.cloned.1.call-start = ((), (), s32[]{:S(2)}) async-start(), calls=%async_computation.12 | async-start | bytes 8650752 | tf_op jit(solution)/shard_map/all_gather | solution.py:143
  9.4 401.0 %all-gather.13.cloned.1.call-start = ((), (), s32[]{:S(2)}) async-start(), calls=%async_computation.9 | async-start | bytes 8650752 | tf_op jit(solution)/shard_map/all_gather | solution.py:145
  10.0 609.5 %all-gather.21.cloned.1.call-start = ((), (), s32[]{:S(2)}) async-start(), calls=%async_computation.13 | async-start | bytes 4325376 | tf_op jit(solution)/shard_map/all_gather | solution.py:147
  10.6 612.4 %all-gather.15.cloned.1.call-start = ((), (), s32[]{:S(2)}) async-start(), calls=%async_computation.10 | async-start | bytes 4325376 | tf_op jit(solution)/shard_map/all_gather | solution.py:146
  11.2 677.8 %all-gather.23.cloned.1.call-start = ((), (), s32[]{:S(2)}) async-start(), calls=%async_computation.15 | async-start | bytes 4325376 | tf_op jit(solution)/shard_map/all_gather | solution.py:148
  11.9 727.6 %all-reduce.17.cloned.1.call-start = ((), (), s32[]{:S(2)}) async-start(), calls=%async_computation.14 | async-start | bytes 524288 | tf_op jit(solution)/shard_map/psum | solution.py:249
  674.6 3.6 collective-permute-start
  676.8 3.9 collective-permute-start.1
  684.4 114.1 %all-gather.25.cloned.1.call-start = ((), (), s32[]{:S(2)}) async-start(), calls=%async_computation.16 | async-start | bytes 2162688 | tf_op jit(solution)/shard_map/all_gather | solution.py:149
  685.2 583.2 %all-reduce.19.cloned.1.call-start = ((), (), s32[]{:S(2)}) async-start(), calls=%async_computation.19 | async-start | bytes 1048576 | tf_op jit(solution)/shard_map/psum | solution.py:311
  807.3 4.1 collective-permute-start.2
  810.0 3.6 collective-permute-start.3
  956.3 751.0 %reduce-scatter.9.cloned.1.call-start = ((), (), s32[]{:S(2)}) async-start(), calls=%async_computation.17 | async-start | bytes 8650752 | tf_op jit(solution)/shard_map/reduce_scatter | solution.py:384
  1251.8 457.3 %reduce-scatter.23.cloned.1.call-start = ((), (), s32[]{:S(2)}) async-start(), calls=%async_computation.25 | async-start | bytes 4325376 | tf_op jit(solution)/shard_map/reduce_scatter | solution.py:381
  1255.7 453.4 %reduce-scatter.21.cloned.1.call-start = ((), (), s32[]{:S(2)}) async-start(), calls=%async_computation.24 | async-start | bytes 8650752 | tf_op jit(solution)/shard_map/reduce_scatter | solution.py:380
  1261.3 573.0 %reduce-scatter.19.cloned.1.call-start = ((), (), s32[]{:S(2)}) async-start(), calls=%async_computation.23 | async-start | bytes 8650752 | tf_op jit(solution)/shard_map/reduce_scatter | solution.py:379
  1268.1 713.7 %reduce-scatter.17.cloned.1.call-start = ((), (), s32[]{:S(2)}) async-start(), calls=%async_computation.22 | async-start | bytes 8650752 | tf_op jit(solution)/shard_map/reduce_scatter | solution.py:378
  1277.4 883.2 %reduce-scatter.13.cloned.1.call-start = ((), (), s32[]{:S(2)}) async-start(), calls=%async_computation.20 | async-start | bytes 16896000 | tf_op jit(solution)/shard_map/reduce_scatter | solution.py:376
  1280.5 343.8 %copy-start.40 = (s32[128]{0:T(128)S(1)}, s32[128]{0:T(128)}, u32[]{:S(2)}) copy-start(s32[128]{0:T(128)} %copy-done.39) | copy-start | bytes 1540
  1636.4 711.4 %reduce-scatter.11.cloned.1.call-start = ((), (), s32[]{:S(2)}) async-start(), calls=%async_computation.18 | async-start | bytes 17301504 | tf_op jit(solution)/shard_map/reduce_scatter | solution.py:385
  1647.1 888.2 %reduce-scatter.15.cloned.1.call-start = ((), (), s32[]{:S(2)}) async-start(), calls=%async_computation.21 | async-start | bytes 17301504 | tf_op jit(solution)/shard_map/reduce_scatter | solution.py:377
  1702.7 832.7 %copy-start.1 = (bf16[4,64,512]{2,1,0:T(8,128)(2,1)S(1)}, bf16[4,64,512]{2,1,0:T(8,128)(2,1)}, u32[]{:S(2)}) copy-start(bf16[4,64,512]{2,1,0:T(8,128)(2,1)} %param.37) | copy-start | bytes 786436
  (64 other events, 1308.1 us)
Sparse Core Ops, SparseCore 0:
  10.9 68.0 all-gather.16
  81.9 89.1 all-gather.10
  174.0 90.4 all-gather.18
  267.2 90.4 all-gather.12
  360.4 60.2 all-gather.20
  423.4 60.8 all-gather.14
  487.1 60.7 all-gather.22
  684.6 54.8 all-reduce.16
  742.7 55.7 all-gather.24
  956.4 53.4 all-reduce.18
  1251.9 147.8 reduce-scatter.8
  1402.5 136.6 reduce-scatter.22
  1542.1 144.8 reduce-scatter.20
  1689.7 144.5 reduce-scatter.18
  1837.0 144.6 reduce-scatter.16
  1984.5 176.0 reduce-scatter.12
  2163.4 184.3 reduce-scatter.10
  2350.6 184.6 reduce-scatter.14
where the time goes:
time: 2570 us; the launch traced here: 2540 us
  waiting for transfers between devices  1180 us (46%)
  matrix products  614 us (24%)
  other arithmetic  395 us (15%)
  local copies, waits for them, and re-layouts  258 us (10%)
  blocking collectives  62.6 us (2%)
    dot_general x53, matrix products, dot_last(): lax.dot_general(left, right, (((left.ndim - 1,), (1,)), ((), ())), prefer...  288 us
    dot_general x54, matrix products, forward_dot(): return jnp.dot(left, right, preferred_element_type=jnp.float32)  269 us
    reduce_scatter x1, waiting for transfers between devices, local(): lax.psum_scatter(grad_dec_rec, ('batch', 'tm'), scatter_dimension=1, tile...  188 us
    reduce_scatter x1, waiting for transfers between devices, local(): lax.psum_scatter(grad_w_rec, ('batch', 'tm'), scatter_dimension=1, tiled=...  187 us
    reduce_scatter x1, waiting for transfers between devices, local(): lax.psum_scatter(grad_table, ('batch', 'tm'), scatter_dimension=1, tiled=...  179 us
    reduce_scatter x1, waiting for transfers between devices, local(): lax.psum_scatter(grad_att_query, ('batch', 'tm'), scatter_dimension=1, ti...  147 us
    reduce_scatter x1, waiting for transfers between devices, local(): lax.psum_scatter(grad_att_key, ('batch', 'tm'), scatter_dimension=1, tile...  125 us
    all_gather x1, waiting for transfers between devices, local(): lax.all_gather(w_rec, ('batch', 'tm'), axis=1, tiled=True)  87.1 us
  transfers between devices with their start and end apart: 22, of which 12 were waited for; matrix products, arithmetic and copies ran while one was open for 44% of the time, Pallas kernels for 0%

commit v1 on v0

v1 whole, which is shorter than its diff:
```python
import functools

import jax
import jax.numpy as jnp
from jax import lax
from jax.experimental import pallas as pl
from jax.experimental.pallas import tpu as pltpu
from jax.sharding import Mesh
from jax.sharding import PartitionSpec as P

BLOCK = 16
LANES = 128
norm_eps = 1e-05
f32 = jnp.float32
bf16 = jnp.bfloat16
CHIPS = ("batch", "chip")
ALL = ("batch", "chip", "core")
VMEM_LIMIT = 60 * 2**20


def sigmoid(v):
    return 0.5 * jnp.tanh(0.5 * v) + 0.5


def forward_dot(left, right):
    return jnp.dot(left, right, preferred_element_type=f32)


def dot_last(left, right):
    return lax.dot_general(left, right, (((left.ndim - 1,), (1,)), ((), ())), preferred_element_type=f32)


def dot_first(left, right):
    return lax.dot_general(left, right, (((0,), (0,)), ((), ())), preferred_element_type=f32)


def params():
    return pltpu.CompilerParams(vmem_limit_bytes=VMEM_LIMIT)


def whole(count, smem_first=True):
    specs = [pl.BlockSpec(memory_space=pltpu.VMEM)] * count
    if smem_first:
        specs[0] = pl.BlockSpec(memory_space=pltpu.SMEM)
    return specs


def dec_forward_kernel(core_ref, table_ref, weight_ref, state_ref, gate_ref, cell_ref):
    steps, hidden = state_ref.shape

    @pl.when(core_ref[0] == 1)
    def _():
        def step(index, carry):
            prev_state, prev_cell = carry
            preact = table_ref[pl.ds(index, 1), :] + forward_dot(prev_state, weight_ref[...])[0:1]
            in_gate = sigmoid(preact[:, :hidden])
            forget = sigmoid(preact[:, hidden : 2 * hidden])
            candidate = jnp.tanh(preact[:, 2 * hidden : 3 * hidden])
            out_gate = sigmoid(preact[:, 3 * hidden :])
            cell = forget * prev_cell + in_gate * candidate
            state = out_gate * jnp.tanh(cell)
            gate_ref[pl.ds(index, 1), :hidden] = in_gate
            gate_ref[pl.ds(index, 1), hidden : 2 * hidden] = forget
            gate_ref[pl.ds(index, 1), 2 * hidden : 3 * hidden] = candidate
            gate_ref[pl.ds(index, 1), 3 * hidden :] = out_gate
            cell_ref[pl.ds(index, 1), :] = cell
            state_ref[pl.ds(index, 1), :] = state
            return (jnp.broadcast_to(state, (16, hidden)).astype(bf16), cell)

        lax.fori_loop(
            0, steps, step, (jnp.zeros((16, hidden), bf16), jnp.zeros((1, hidden), f32))
        )

    @pl.when(core_ref[0] != 1)
    def _():
        state_ref[...] = jnp.zeros_like(state_ref)
        gate_ref[...] = jnp.zeros_like(gate_ref)
        cell_ref[...] = jnp.zeros_like(cell_ref)


def dec_forward(core, table_rows, weight):
    steps, width = table_rows.shape
    hidden = width // 4
    return pl.pallas_call(
        dec_forward_kernel,
        in_specs=whole(3),
        out_shape=[
            jax.ShapeDtypeStruct((steps, hidden), f32),
            jax.ShapeDtypeStruct((steps, width), f32),
            jax.ShapeDtypeStruct((steps, hidden), f32),
        ],
        compiler_params=params(),
        name="dec_forward",
    )(core, table_rows, weight)


def transpose_into(target_ref, weight_ref):
    width = weight_ref.shape[1]

    def part(index, carry):
        start = pl.multiple_of(index * 256, 256)
        target_ref[pl.ds(start, 256), :] = weight_ref[:, pl.ds(start, 256)].T
        return carry

    lax.fori_loop(0, width // 256, part, 0)


def dec_backward_kernel(core_ref, gate_ref, cell_ref, grad_ref, weight_ref, out_ref, turned_ref):
    steps, hidden = grad_ref.shape

    @pl.when(core_ref[0] == 1)
    def _():
        transpose_into(turned_ref, weight_ref)

        def step(back, carry):
            rec_grad, cell_grad = carry
            index = steps - 1 - back
            row = pl.ds(index, 1)
            in_gate = gate_ref[row, :hidden]
            forget = gate_ref[row, hidden : 2 * hidden]
            candidate = gate_ref[row, 2 * hidden : 3 * hidden]
            out_gate = gate_ref[row, 3 * hidden :]
            prev_cell = jnp.where(index > 0, cell_ref[pl.ds(jnp.maximum(index - 1, 0), 1), :], 0.0)
            squashed = jnp.tanh(cell_ref[row, :])
            state_grad = grad_ref[row, :] + rec_grad
            cell_grad = cell_grad + state_grad * out_gate * (1.0 - squashed * squashed)
            pre_grad = jnp.concatenate(
                [
                    cell_grad * candidate * in_gate * (1.0 - in_gate),
                    cell_grad * prev_cell * forget * (1.0 - forget),
                    cell_grad * in_gate * (1.0 - candidate * candidate),
                    state_grad * squashed * out_gate * (1.0 - out_gate),
                ],
                axis=1,
            )
            out_ref[row, :] = pre_grad
            low = jnp.broadcast_to(pre_grad, (16, 4 * hidden)).astype(bf16)
            return (forward_dot(low, turned_ref[...])[0:1], cell_grad * forget)

        zero = jnp.zeros((1, hidden), f32)
        lax.fori_loop(0, steps, step, (zero, zero))

    @pl.when(core_ref[0] != 1)
    def _():
        out_ref[...] = jnp.zeros_like(out_ref)


def dec_backward(core, gates, cells, state_grad, weight):
    steps, hidden = state_grad.shape
    return pl.pallas_call(
        dec_backward_kernel,
        in_specs=whole(5),
        out_shape=jax.ShapeDtypeStruct((steps, 4 * hidden), f32),
        scratch_shapes=[pltpu.VMEM((4 * hidden, hidden), bf16)],
        compiler_params=params(),
        name="dec_backward",
    )(core, gates, cells, state_grad, weight)


def enc_forward_kernel(
    core_ref,
    frame_ref,
    in_ref,
    weight_ref,
    gain_ref,
    shift_ref,
    init_ref,
    hidden_ref,
    norm_ref,
    cell_ref,
    scale_ref,
):
    steps, rows, hidden = hidden_ref.shape
    width = 4 * hidden

    @pl.when(core_ref[0] == 0)
    def _():
        def feed(index, carry):
            columns = pl.ds(pl.multiple_of(index * 512, 512), 512)
            part = forward_dot(frame_ref[...], in_ref[:, columns])
            norm_ref[:, :, columns] = part.reshape(steps, rows, 512)
            return carry

        lax.fori_loop(0, width // 512, feed, 0)

        def step(index, carry):
            prev_hidden, prev_cell = carry
            preact = norm_ref[index] + forward_dot(prev_hidden, weight_ref[...])
            centred = preact - jnp.mean(preact, axis=-1, keepdims=True)
            scale = lax.rsqrt(jnp.mean(centred * centred, axis=-1, keepdims=True) + norm_eps)
            normed = centred * scale
            norm_ref[index] = normed
            scale_ref[index] = jnp.broadcast_to(scale, (rows, LANES))

            def gate(which):
                columns = slice(which * hidden, (which + 1) * hidden)
                return normed[:, columns] * gain_ref[:, columns] + shift_ref[:, columns]

            cell = sigmoid(gate(1)) * prev_cell + sigmoid(gate(0)) * jnp.tanh(gate(2))
            state = (sigmoid(gate(3)) * jnp.tanh(cell)).astype(bf16)
            cell_ref[index] = cell
            hidden_ref[index] = state
            return (state, cell)

        start = (
            jnp.broadcast_to(init_ref[0:1, :], (rows, hidden)).astype(bf16),
            jnp.broadcast_to(init_ref[1:2, :], (rows, hidden)),
        )
        lax.fori_loop(0, steps, step, start)

    @pl.when(core_ref[0] != 0)
    def _():
        hidden_ref[...] = jnp.zeros_like(hidden_ref)


def enc_forward(core, frame_rows, w_in, w_rec, gain, shift, init_state):
    hidden = w_rec.shape[0]
    steps, rows = BLOCK, frame_rows.shape[0] // BLOCK
    return pl.pallas_call(
        enc_forward_kernel,
        in_specs=whole(7),
        out_shape=[
            jax.ShapeDtypeStruct((steps, rows, hidden), bf16),
            jax.ShapeDtypeStruct((steps, rows, 4 * hidden), f32),
            jax.ShapeDtypeStruct((steps, rows, hidden), f32),
            jax.ShapeDtypeStruct((steps, rows, LANES), f32),
        ],
        compiler_params=params(),
        name="enc_forward",
    )(core, frame_rows, w_in, w_rec, gain, shift, init_state)


def enc_backward_kernel(
    core_ref,
    norm_ref,
    cell_ref,
    scale_ref,
    grad_ref,
    weight_ref,
    gain_ref,
    shift_ref,
    init_ref,
    out_ref,
    gain_grad_ref,
    shift_grad_ref,
    init_grad_ref,
    turned_ref,
    gain_sum,
    shift_sum,
):
    steps, rows, hidden = grad_ref.shape
    width = 4 * hidden

    @pl.when(core_ref[0] == 0)
    def _():
        transpose_into(turned_ref, weight_ref)
        gain_sum[...] = jnp.zeros_like(gain_sum)
        shift_sum[...] = jnp.zeros_like(shift_sum)

        def step(back, carry):
            rec_grad, cell_grad = carry
            index = steps - 1 - back

            def gate(which):
                columns = slice(which * hidden, (which + 1) * hidden)
                return norm_ref[index, :, columns] * gain_ref[:, columns] + shift_ref[:, columns]

            in_gate, forget = (sigmoid(gate(0)), sigmoid(gate(1)))
            candidate, out_gate = (jnp.tanh(gate(2)), sigmoid(gate(3)))
            start_cell = jnp.broadcast_to(init_ref[1:2, :], (rows, hidden))
            prev_cell = jnp.where(index > 0, cell_ref[jnp.maximum(index - 1, 0)], start_cell)
            squashed = jnp.tanh(cell_ref[index])
            state_grad = grad_ref[index] + rec_grad
            cell_grad = cell_grad + state_grad * out_gate * (1.0 - squashed * squashed)
            gate_grad = jnp.concatenate(
                [
                    cell_grad * candidate * in_gate * (1.0 - in_gate),
                    cell_grad * prev_cell * forget * (1.0 - forget),
                    cell_grad * in_gate * (1.0 - candidate * candidate),
                    state_grad * squashed * out_gate * (1.0 - out_gate),
                ],
                axis=1,
            )
            normed = norm_ref[index]
            gain_sum[...] += jnp.sum((gate_grad * normed).reshape(rows // 8, 8, width), axis=0)
            shift_sum[...] += jnp.sum(gate_grad.reshape(rows // 8, 8, width), axis=0)
            scaled = gate_grad * gain_ref[...]
            mean_grad = jnp.mean(scaled, axis=-1, keepdims=True)
            mean_normed = jnp.mean(scaled * normed, axis=-1, keepdims=True)
            pre_grad = scale_ref[index, :, 0:1] * (scaled - mean_grad - normed * mean_normed)
            low = pre_grad.astype(bf16)
            out_ref[index] = low
            return (forward_dot(low, turned_ref[...]), cell_grad * forget)

        zero = jnp.zeros((rows, hidden), f32)
        hidden_grad, cell_grad = lax.fori_loop(0, steps, step, (zero, zero))
        gain_grad_ref[...] = jnp.sum(gain_sum[...], axis=0, keepdims=True)
        shift_grad_ref[...] = jnp.sum(shift_sum[...], axis=0, keepdims=True)
        init_grad_ref[0:1, :] = jnp.sum(hidden_grad, axis=0, keepdims=True)
        init_grad_ref[1:2, :] = jnp.sum(cell_grad, axis=0, keepdims=True)

    @pl.when(core_ref[0] != 0)
    def _():
        out_ref[...] = jnp.zeros_like(out_ref)
        gain_grad_ref[...] = jnp.zeros_like(gain_grad_ref)
        shift_grad_ref[...] = jnp.zeros_like(shift_grad_ref)
        init_grad_ref[...] = jnp.zeros_like(init_grad_ref)


def enc_backward(core, normed, cells, scales, memory_grad, w_rec, gain, shift, init_state):
    steps, rows, hidden = memory_grad.shape
    return pl.pallas_call(
        enc_backward_kernel,
        in_specs=whole(9),
        out_shape=[
            jax.ShapeDtypeStruct((steps, rows, 4 * hidden), bf16),
            jax.ShapeDtypeStruct((1, 4 * hidden), f32),
            jax.ShapeDtypeStruct((1, 4 * hidden), f32),
            jax.ShapeDtypeStruct((2, hidden), f32),
        ],
        scratch_shapes=[
            pltpu.VMEM((4 * hidden, hidden), bf16),
            pltpu.VMEM((8, 4 * hidden), f32),
            pltpu.VMEM((8, 4 * hidden), f32),
        ],
        compiler_params=params(),
        name="enc_backward",
    )(core, normed, cells, scales, memory_grad, w_rec, gain, shift, init_state)


def moved(value, by, fill):
    count = value.shape[1]
    lane = lax.broadcasted_iota(jnp.int32, value.shape, 1)
    rolled = pltpu.roll(value, by % count, 1)
    inside = lane >= by if by > 0 else lane < count + by
    return jnp.where(inside, rolled, fill)


def spans(count):
    sizes, size = ([], 1)
    while size < count:
        sizes.append(size)
        size *= 2
    return sizes


def attend_kernel(
    scalar_ref,
    length_ref,
    query_ref,
    key_ref,
    vec_ref,
    noise_ref,
    memory_ref,
    raw_ref,
    sig_ref,
    before_ref,
    align_ref,
    share_ref,
    weight_ref,
    context_ref,
    column_ref,
):
    steps, count = noise_ref.shape
    half = vec_ref.shape[1]
    lane = lax.broadcasted_iota(jnp.int32, (64, LANES), 1)

    def rows_loop(block, carry):
        rows = pl.ds(pl.multiple_of(block * 64, 64), 64)
        found = jnp.zeros((64, LANES), f32)
        for kind in range(2):

            def one(index, found):
                total = jnp.zeros((64, LANES), f32)
                for tile in range(half // LANES):
                    columns = pl.ds(kind * half + tile * LANES, LANES)
                    act = jnp.tanh(key_ref[rows, columns] + query_ref[index, :, columns])
                    total += act * vec_ref[kind : kind + 1, pl.ds(tile * LANES, LANES)]
                energy = jnp.sum(total, axis=1, keepdims=True)
                return jnp.where(lane == kind * steps + index, energy, found)

            found = lax.fori_loop(0, steps, one, found)
        column_ref[rows, :] = found
        return carry

    lax.fori_loop(0, count // 64, rows_loop, 0)
    energies = column_ref[...].T
    raw = energies[:steps]
    span = energies[steps : 2 * steps]
    position = lax.broadcasted_iota(jnp.int32, (steps, count), 1)
    mask = (position < length_ref[0]).astype(f32)
    sig = sigmoid(raw * scalar_ref[0] + scalar_ref[1] + noise_ref[...])
    stop = sig * mask
    survive = 1.0 - stop
    for size in spans(count):
        survive = survive * moved(survive, size, 1.0)
    before = moved(survive, 1, 1.0)
    align = stop * before
    share = jnp.where(position == 0, 1.0, sigmoid(span - moved(span, 1, 0.0)))
    weight = align * share + moved(align, -1, 0.0) * (1.0 - moved(share, -1, 1.0))
    raw_ref[...] = raw
    sig_ref[...] = sig
    before_ref[...] = before
    align_ref[...] = align
    share_ref[...] = share
    low = weight.astype(bf16)
    weight_ref[...] = low
    context_ref[...] = forward_dot(low, memory_ref[...]).astype(bf16)


def attend(scalars, length, queries, keys, att_vec, noise, memory):
    steps, count = noise.shape
    grid = jax.ShapeDtypeStruct((steps, count), f32)
    specs = whole(7)
    specs[1] = pl.BlockSpec(memory_space=pltpu.SMEM)
    return pl.pallas_call(
        attend_kernel,
        in_specs=specs,
        out_shape=[grid] * 5
        + [
            jax.ShapeDtypeStruct((steps, count), bf16),
            jax.ShapeDtypeStruct((steps, memory.shape[1]), bf16),
        ],
        scratch_shapes=[pltpu.VMEM((count, LANES), f32)],
        compiler_params=params(),
        name="attend",
    )(scalars, length, queries[:, None, :], keys, att_vec, noise, memory)


def attend_back_kernel(
    scalar_ref,
    length_ref,
    grad_ref,
    memory_ref,
    raw_ref,
    sig_ref,
    before_ref,
    align_ref,
    share_ref,
    query_ref,
    key_ref,
    vec_ref,
    key_grad_ref,
    query_grad_ref,
    vec_grad_ref,
    mono_ref,
    wide_ref,
    query_sum,
    vec_sum,
):
    steps, count = raw_ref.shape
    half = vec_ref.shape[1]
    position = lax.broadcasted_iota(jnp.int32, (steps, count), 1)
    mask = (position < length_ref[0]).astype(f32)
    sig, before, align, share = (sig_ref[...], before_ref[...], align_ref[...], share_ref[...])
    stop = sig * mask
    weight_grad = dot_last(grad_ref[...], memory_ref[...])
    prev_grad = moved(weight_grad, 1, 0.0)
    align_grad = weight_grad * share + prev_grad * (1.0 - share)
    term = align * (weight_grad - prev_grad) * share * (1.0 - share)
    span_grad = term - moved(term, -1, 0.0)
    later = align_grad * stop
    keep = 1.0 - stop
    for size in spans(count):
        later = later + keep * moved(later, -size, 0.0)
        keep = keep * moved(keep, -size, 1.0)
    stop_grad = before * (align_grad - moved(later, -1, 0.0))
    energy_grad = stop_grad * sig * (1.0 - sig) * mask
    raw_grad = energy_grad * scalar_ref[0]
    gain_part = jnp.sum(jnp.sum(energy_grad * raw_ref[...], axis=1, keepdims=True), axis=0, keepdims=True)
    shift_part = jnp.sum(jnp.sum(energy_grad, axis=1, keepdims=True), axis=0, keepdims=True)
    spot = lax.broadcasted_iota(jnp.int32, (1, LANES), 1)
    mono_ref[...] = jnp.where(spot == 0, gain_part, jnp.where(spot == 1, shift_part, 0.0))
    padding = jnp.zeros((LANES - 2 * steps, count), f32)
    columns_of = jnp.concatenate([raw_grad, span_grad, padding], axis=0).T
    for which in range(2 * steps):
        wide_ref[which] = jnp.broadcast_to(columns_of[:, which : which + 1], (count, LANES))
    query_sum[...] = jnp.zeros_like(query_sum)
    for kind in range(2):

        def tile_loop(tile, carry):
            columns = pl.ds(pl.multiple_of(kind * half + tile * LANES, LANES), LANES)
            vec_columns = pl.ds(pl.multiple_of(tile * LANES, LANES), LANES)
            vec = vec_ref[kind : kind + 1, vec_columns]

            def rows_loop(block, vec_part):
                rows = pl.ds(pl.multiple_of(block * 64, 64), 64)
                keys = key_ref[rows, columns]

                def one(index, carry):
                    key_part, vec_part = carry
                    act = jnp.tanh(keys + query_ref[index, :, columns])
                    wide = wide_ref[kind * steps + index, rows, :]
                    product = wide * act
                    slope = wide - product * act
                    folded = jnp.sum(slope.reshape(8, 8, LANES), axis=0)
                    query_sum[index, :, columns] += folded
                    return (key_part + slope, vec_part + jnp.sum(product.reshape(8, 8, LANES), axis=0))

                key_part, vec_part = lax.fori_loop(
                    0, steps, one, (jnp.zeros((64, LANES), f32), vec_part), unroll=2
                )
                key_grad_ref[rows, columns] = (key_part * vec).astype(bf16)
                return vec_part

            vec_part = lax.fori_loop(0, count // 64, rows_loop, jnp.zeros((8, LANES), f32))
            vec_sum[:, columns] = vec_part
            return carry

        lax.fori_loop(0, half // LANES, tile_loop, 0)
        vec_grad_ref[kind : kind + 1, :] = jnp.sum(
            vec_sum[:, kind * half : (kind + 1) * half], axis=0, keepdims=True
        )
    for index in range(steps):
        total = jnp.sum(query_sum[index], axis=0, keepdims=True)
        for kind in range(2):
            columns = slice(kind * half, (kind + 1) * half)
            query_grad_ref[index : index + 1, columns] = total[:, columns] * vec_ref[kind : kind + 1, :]


def attend_back(scalars, length, context_grad, memory, saved, queries, keys, att_vec):
    steps, count = saved[0].shape
    width = queries.shape[1]
    specs = whole(12)
    specs[1] = pl.BlockSpec(memory_space=pltpu.SMEM)
    return pl.pallas_call(
        attend_back_kernel,
        in_specs=specs,
        out_shape=[
            jax.ShapeDtypeStruct((count, width), bf16),
            jax.ShapeDtypeStruct((steps, width), f32),
            jax.ShapeDtypeStruct((2, width // 2), f32),
            jax.ShapeDtypeStruct((1, LANES), f32),
        ],
        scratch_shapes=[
            pltpu.VMEM((2 * steps, count, LANES), f32),
            pltpu.VMEM((steps, 8, width), f32),
            pltpu.VMEM((8, width), f32),
        ],
        compiler_params=params(),
        name="attend_back",
    )(scalars, length, context_grad, memory, *saved, queries[:, None, :], keys, att_vec)


def head_kernel(
    state_ref,
    context_ref,
    label_ref,
    mask_ref,
    proj_ref,
    proj_b_ref,
    out_w_ref,
    out_b_ref,
    loss_ref,
    out_b_grad_ref,
    proj_b_grad_ref,
    proj_low_ref,
    logit_low_ref,
    proj_grad_ref,
    state_grad_ref,
    context_grad_ref,
):
    hidden = state_ref.shape[1]
    rows, vocab = logit_low_ref.shape
    proj_out = jnp.tanh(
        forward_dot(state_ref[...], proj_ref[:hidden, :])
        + forward_dot(context_ref[...], proj_ref[hidden:, :])
        + proj_b_ref[...]
    )
    proj_low = proj_out.astype(bf16)
    proj_low_ref[...] = proj_low
    logits = forward_dot(proj_low, out_w_ref[...]) + out_b_ref[...]
    top = jnp.max(logits, axis=1, keepdims=True)
    powers = jnp.exp(logits - top)
    total = jnp.sum(powers, axis=1, keepdims=True)
    target = lax.broadcasted_iota(jnp.int32, (rows, vocab), 1) == label_ref[...]
    picked = jnp.sum(jnp.where(target, logits, 0.0), axis=1, keepdims=True)
    mask = mask_ref[...]
    loss_ref[...] = jnp.broadcast_to((jnp.log(total) + top - picked) * mask, (rows, LANES))
    logit_grad = (powers / total - target.astype(f32)) * mask
    out_b_grad_ref[...] = jnp.sum(logit_grad, axis=0, keepdims=True)
    logit_low = logit_grad.astype(bf16)
    logit_low_ref[...] = logit_low
    proj_grad = dot_last(logit_low, out_w_ref[...]) * (1.0 - proj_out * proj_out)
    proj_b_grad_ref[...] = jnp.sum(proj_grad, axis=0, keepdims=True)
    proj_grad_low = proj_grad.astype(bf16)
    proj_grad_ref[...] = proj_grad_low
    state_grad_ref[...] = dot_last(proj_grad_low, proj_ref[:hidden, :])
    context_grad_ref[...] = dot_last(proj_grad_low, proj_ref[hidden:, :]).astype(bf16)


def head(states, context, label_column, mask_column, proj_w, proj_b, out_w, out_b):
    rows, hidden = states.shape
    units = proj_w.shape[1]
    vocab = out_w.shape[1]
    return pl.pallas_call(
        head_kernel,
        in_specs=whole(8, False),
        out_shape=[
            jax.ShapeDtypeStruct((rows, LANES), f32),
            jax.ShapeDtypeStruct((1, vocab), f32),
            jax.ShapeDtypeStruct((1, units), f32),
            jax.ShapeDtypeStruct((rows, units), bf16),
            jax.ShapeDtypeStruct((rows, vocab), bf16),
            jax.ShapeDtypeStruct((rows, units), bf16),
            jax.ShapeDtypeStruct((rows, hidden), f32),
            jax.ShapeDtypeStruct((rows, hidden), bf16),
        ],
        compiler_params=params(),
        name="head",
    )(states, context, label_column, mask_column, proj_w, proj_b, out_w, out_b)


def swap(value):
    return lax.ppermute(value, "core", [(0, 1), (1, 0)])


def to_core(value, core):
    return lax.ppermute(value, "core", [(1 - core, core)])


def gather_columns(shard):
    return lax.all_gather(shard, ALL, axis=1, tiled=True)


def local(
    frames,
    noise,
    frame_lengths,
    labels,
    label_lengths,
    w_in,
    w_rec,
    ln_gain,
    ln_shift,
    init_state,
    dec_table,
    dec_rec,
    att_query,
    att_key,
    att_bias,
    att_vec,
    monotonic,
    proj_w,
    proj_b,
    out_w,
    out_b,
):
    core, chip, plane = (lax.axis_index("core"), lax.axis_index("chip"), lax.axis_index("batch"))
    planes, plane_chips = (lax.axis_size("batch"), lax.axis_size("chip"))
    chips = planes * plane_chips
    line = 2 * plane_chips
    utterances, slice_frames, feat = frames.shape
    label_steps = labels.shape[1]
    hidden = w_rec.shape[0]
    width = 4 * hidden
    vocab = out_b.shape[0]
    sharers = line // utterances
    chip_sharers = sharers // 2
    own_steps = label_steps // sharers
    utterance = chip // chip_sharers
    part = chip % chip_sharers
    share = part * 2 + core
    all_frames = line * slice_frames
    enc_frames = all_frames // chip_sharers
    on_enc = core == 0
    core_arg = core.astype(jnp.int32).reshape(1)
    gain_row, shift_row = (ln_gain.reshape(1, -1), ln_shift.reshape(1, -1))

    all_labels = lax.all_gather(labels, "batch", axis=0, tiled=True)
    prev_ids = jnp.concatenate(
        [jnp.zeros((planes * utterances, 1), jnp.int32), all_labels[:, :-1]], axis=1
    )
    onehot = (prev_ids.reshape(-1)[:, None] == jnp.arange(vocab)[None, :]).astype(bf16)
    rows_here = forward_dot(onehot, dec_table).astype(bf16).reshape(planes * utterances, label_steps, -1)
    rows_here = jnp.repeat(rows_here, chip_sharers, axis=0)
    rows_mine = lax.all_to_all(rows_here, CHIPS, 0, 0, tiled=True)
    rows_other = swap(rows_mine)
    low_rows = jnp.where(on_enc, rows_mine, rows_other)
    high_rows = jnp.where(on_enc, rows_other, rows_mine)
    table_rows = jnp.stack([low_rows, high_rows], axis=1)
    table_rows = table_rows.transpose(2, 0, 1, 3).reshape(label_steps, width).astype(f32)

    full_dec = gather_columns(dec_rec)
    states_dec, dec_gates, dec_cells = dec_forward(core_arg, table_rows, full_dec)

    if chip_sharers == 1:
        pieces = frames.reshape(utterances, slice_frames, feat)
        pieces = pieces.reshape(utterances, 2, slice_frames // 2, feat).reshape(line, slice_frames // 2, feat)
        got = lax.all_to_all(pieces, ("chip", "core"), 0, 0, tiled=True)
        other = to_core(got, 0)
        enc_in = jnp.stack([got, other], axis=1).reshape(enc_frames, feat)
    else:
        got = lax.all_gather(frames, ("chip", "core"), axis=0)
        got = lax.dynamic_index_in_dim(got, utterance, 1, keepdims=False).reshape(all_frames, feat)
        enc_in = lax.dynamic_slice_in_dim(got, part * enc_frames, enc_frames, axis=0)
    enc_rows = enc_frames // BLOCK
    frame_rows = enc_in.reshape(enc_rows, BLOCK, feat).transpose(1, 0, 2).reshape(enc_frames, feat)
    noise_pieces = noise.reshape(line, own_steps, slice_frames)
    noise_own = lax.all_to_all(noise_pieces, ("chip", "core"), 0, 0, tiled=True)
    noise_own = noise_own.transpose(1, 0, 2).reshape(own_steps, all_frames)

    full_in, full_rec = (gather_columns(w_in), gather_columns(w_rec))
    enc_hidden, enc_norm, enc_cell, enc_scale = enc_forward(
        core_arg, frame_rows, full_in, full_rec, gain_row, shift_row, init_state
    )
    memory_part = enc_hidden.transpose(1, 0, 2).reshape(enc_frames, hidden)
    memory = jnp.where(on_enc, memory_part, to_core(memory_part, 1))
    if chip_sharers > 1:
        groups = [
            [first * chip_sharers + i for i in range(chip_sharers)] for first in range(utterances)
        ]
        memory = lax.all_gather(memory, "chip", axis=0, tiled=True, axis_index_groups=groups)

    full_query, full_key = (gather_columns(att_query), gather_columns(att_key))
    full_proj = gather_columns(proj_w)
    full_out = lax.all_gather(out_w, ALL, axis=0, tiled=True)

    states_low = states_dec.astype(bf16)
    states_all = jnp.where(on_enc, to_core(states_low, 0), states_low)
    states_own = lax.dynamic_slice_in_dim(states_all, share * own_steps, own_steps, axis=0)
    queries = forward_dot(states_own, full_query) + att_bias.reshape(1, -1)
    keys = forward_dot(memory, full_key)

    norm_inv = lax.rsqrt(jnp.sum(att_vec[0] * att_vec[0]) + 1e-06)
    scalars = jnp.stack([monotonic[0] * norm_inv, monotonic[1]])
    length = lax.dynamic_slice_in_dim(frame_lengths, utterance, 1)
    attended = attend(scalars, length, queries, keys, att_vec, noise_own, memory)
    saved, weight_low, context = (attended[:5], attended[5], attended[6])

    label_row = lax.dynamic_slice(labels, (utterance, share * own_steps), (1, own_steps))
    label_length = lax.dynamic_slice_in_dim(label_lengths, utterance, 1)
    step_ids = share * own_steps + jnp.arange(own_steps)
    mask_column = (step_ids < label_length).astype(f32).reshape(own_steps, 1)
    loss_rows, out_b_grad, proj_b_grad, proj_low, logit_low, proj_grad_low, state_head, context_grad = head(
        states_own,
        context,
        label_row.reshape(own_steps, 1),
        mask_column,
        full_proj,
        proj_b.reshape(1, -1),
        full_out,
        out_b.reshape(1, -1),
    )

    key_low, query_grad, vec_raw, mono_parts = attend_back(
        scalars, length, context_grad, memory, saved, queries, keys, att_vec
    )
    query_low = query_grad.astype(bf16)
    bias_grad = jnp.sum(query_grad, axis=0).reshape(2, -1)
    gain_part = mono_parts[0, 0]
    vec_fix = -gain_part * monotonic[0] * norm_inv * norm_inv * norm_inv
    vec_grad = vec_raw.at[0].add(vec_fix * att_vec[0])
    mono_grad = jnp.stack([gain_part * norm_inv, mono_parts[0, 1]])

    memory_grad = dot_first(weight_low, context_grad) + dot_last(key_low, full_key)
    att_key_part = dot_first(memory, key_low).astype(bf16)
    if chip_sharers > 1:
        memory_grad = lax.psum_scatter(
            memory_grad, "chip", scatter_dimension=0, tiled=True, axis_index_groups=groups
        )
    memory_grad = memory_grad + to_core(memory_grad.astype(bf16), 0).astype(f32)
    memory_steps = memory_grad.reshape(enc_rows, BLOCK, hidden).transpose(1, 0, 2)

    state_grad = state_head + dot_last(query_low, full_query)
    both = jnp.stack([to_core(state_grad, 1), state_grad]).reshape(2 * own_steps, hidden)
    if chip_sharers > 1:
        both = lax.all_gather(both, "chip", axis=0, tiled=True, axis_index_groups=groups)

    enc_grad, gain_grad, shift_grad, init_grad = enc_backward(
        core_arg, enc_norm, enc_cell, enc_scale, memory_steps, full_rec, gain_row, shift_row, init_state
    )
    dec_grad = dec_backward(core_arg, dec_gates, dec_cells, both, full_dec)

    enc_grad_rows = enc_grad.reshape(enc_frames, width)
    start_hidden = jnp.broadcast_to(init_state[0].astype(bf16), (1, enc_rows, hidden))
    prev_hidden = jnp.concatenate([start_hidden, enc_hidden[:-1]], axis=0).reshape(enc_frames, hidden)
    rec_part = dot_first(prev_hidden, enc_grad_rows).astype(bf16)
    in_part = dot_first(frame_rows, enc_grad_rows).astype(bf16)
    w_rec_out = lax.psum_scatter(rec_part, ALL, scatter_dimension=1, tiled=True).astype(f32)
    w_in_out = lax.psum_scatter(in_part, ALL, scatter_dimension=1, tiled=True).astype(f32)
    key_out = lax.psum_scatter(att_key_part, ALL, scatter_dimension=1, tiled=True).astype(f32)

    frames_part = dot_last(enc_grad_rows, full_in).astype(bf16)
    frames_part = frames_part.reshape(BLOCK, enc_rows, feat).transpose(1, 0, 2).reshape(enc_frames, feat)
    if chip_sharers == 1:
        halves = frames_part.reshape(line, 2, slice_frames // 2, feat)
        mine = jnp.where(on_enc, halves[:, 0], to_core(halves[:, 1], 1))
        back = lax.all_to_all(mine, ("chip", "core"), 0, 0, tiled=True)
        frames_grad = back.reshape(utterances, slice_frames, feat).astype(f32)
    else:
        everyone = lax.all_gather(frames_part, ("chip", "core"), axis=0)
        everyone = everyone.reshape(utterances, chip_sharers, 2, enc_frames, feat)[:, :, 0]
        everyone = everyone.reshape(utterances, all_frames, feat)
        at = (chip * 2 + core) * slice_frames
        frames_grad = lax.dynamic_slice_in_dim(everyone, at, slice_frames, axis=1).astype(f32)

    row_parts = jnp.concatenate([states_own, context, logit_low], axis=1)
    row_all = lax.all_gather(row_parts, ALL, axis=0, tiled=True)
    rows_total = row_all.shape[0]
    states_rows = row_all[:, :hidden]
    joined_rows = row_all[:, : 2 * hidden]
    logit_rows = row_all[:, 2 * hidden :]
    by_utt = states_rows.reshape(planes * utterances, label_steps, hidden)
    states_prev = jnp.concatenate([jnp.zeros_like(by_utt[:, :1]), by_utt[:, :-1]], axis=1)
    states_prev = states_prev.reshape(rows_total, hidden)

    def for_chips(value):
        pair = jnp.concatenate([value, to_core(value, 0)], axis=0)
        return pair.reshape(2 * own_steps, chips, -1).transpose(1, 0, 2)

    head_pack = jnp.concatenate(
        [for_chips(query_low), for_chips(proj_grad_low), for_chips(proj_low)], axis=2
    )
    dec_own = lax.dynamic_slice_in_dim(dec_grad, part * 2 * own_steps, 2 * own_steps, axis=0)
    dec_pack = dec_own.astype(bf16).reshape(2 * own_steps, chips, -1).transpose(1, 0, 2)
    pack = lax.all_to_all(jnp.where(on_enc, head_pack, dec_pack), CHIPS, 0, 0, tiled=True)
    pack = pack.reshape(rows_total, -1)
    query_cols = 2 * att_query.shape[1]
    proj_cols = 2 * proj_w.shape[1]
    query_pair = dot_first(states_rows, pack[:, :query_cols])
    proj_pair = dot_first(joined_rows, pack[:, query_cols : query_cols + proj_cols])
    out_pair = dot_first(pack[:, query_cols + proj_cols :], logit_rows)
    rec_pair = dot_first(states_prev, pack)
    table_pair = dot_first(onehot, pack)

    def settle(pair, axis, owner):
        low, high = jnp.split(pair, 2, axis=axis)
        if owner == 0:
            return jnp.where(on_enc, low, to_core(high, 1))
        return jnp.where(on_enc, to_core(low, 0), high)

    query_out = settle(query_pair, 1, 0)
    proj_w_out = settle(proj_pair, 1, 0)
    out_w_out = settle(out_pair, 0, 0)
    dec_rec_out = settle(rec_pair, 1, 1)
    table_out = settle(table_pair, 1, 1)

    loss_out, init_out, gain_out, shift_out, bias_out, vec_out, mono_out, proj_b_out, out_b_out = lax.psum(
        (
            jnp.sum(loss_rows[:, 0]),
            init_grad,
            gain_grad.reshape(-1),
            shift_grad.reshape(-1),
            bias_grad,
            vec_grad,
            mono_grad,
            proj_b_grad.reshape(-1),
            out_b_grad.reshape(-1),
        ),
        ALL,
    )
    return (
        loss_out,
        frames_grad,
        w_in_out,
        w_rec_out,
        gain_out,
        shift_out,
        init_out,
        table_out,
        dec_rec_out,
        query_out,
        key_out,
        bias_out,
        vec_out,
        mono_out,
        proj_w_out,
        proj_b_out,
        out_w_out,
        out_b_out,
    )


def solution(mesh):
    planes, line = mesh.devices.shape
    fine = Mesh(mesh.devices.reshape(planes, line // 2, 2), ALL)
    tm = ("chip", "core")
    columns = P(None, ALL)
    return jax.shard_map(
        local,
        mesh=fine,
        in_specs=(
            P("batch", tm, None),
            P("batch", None, tm),
            P("batch"),
            P("batch", None),
            P("batch"),
            columns,
            columns,
            P(),
            P(),
            P(),
            columns,
            columns,
            columns,
            columns,
            P(),
            P(),
            P(),
            columns,
            P(),
            P(ALL, None),
            P(),
        ),
        out_specs=(
            P(),
            P("batch", tm, None),
            columns,
            columns,
            P(),
            P(),
            P(),
            columns,
            columns,
            columns,
            columns,
            P(),
            P(),
            P(),
            columns,
            P(),
            P(ALL, None),
            P(),
        ),
        check_vma=False,
    )
```

time: 2570 us -> 1030 us (0.40)
  waiting for transfers between devices: 1180 us -> 562 us
  matrix products: 614 us -> 53.4 us
  other arithmetic: 395 us -> 20.3 us
  local copies, waits for them, and re-layouts: 258 us -> 46.3 us
  Pallas kernels: 0 us -> 182 us
  starting transfers between devices: 9.39 us -> 85.6 us
    reduce_scatter x8 -> x1, waiting for transfers between devices: 826 us -> 0.01 us  [local(): lax.psum_scatter(att_key_part, ALL, scatter_dimension=1, tiled=True)]
    dot_general x58 -> x3, matrix products: 286 us -> 11.1 us  [forward_dot(): return jnp.dot(left, right, preferred_element_type=f32)]
    dot_general x53 -> x3, matrix products: 288 us -> 13.3 us  [dot_last(): lax.dot_general(left, right, (((left.ndim - 1,), (1,)), ((), ())), prefer...]
    unnamed x18 -> x13, waiting for transfers between devices: 5.18 us -> 191 us
    pallas_call x0 -> x7, Pallas kernels: none -> 182 us  [the longest x1 45.8 us: enc_backward(): pl.pallas_call(enc_backward_kernel, in_specs=whole(9), out_shape=[jax.Sha...]
    reduce_sum x115 -> x2, other arithmetic: 153 us -> 1.91 us  [the longest x1 1.31 us: local(): norm_inv = lax.rsqrt(jnp.sum(att_vec[0] * att_vec[0]) + 1e-06)]
    dynamic_update_slice x136 -> x0, local copies, waits for them, and re-layouts: 124 us -> none  [the longest x64 62.8 us: local(): lax.scan(dec_step, (zero_state.astype(jnp.bfloat16), zero_state), jnp.swa...]
    dynamic_update_slice x144 -> x0, other arithmetic: 99.9 us -> none  [the longest x64 40.6 us: local(): lax.scan(dec_step, (zero_state.astype(jnp.bfloat16), zero_state), jnp.swa...]
  transfers between devices with their start and end apart: 22 -> 31, of which waited for: 12 -> 15; matrix products, arithmetic and copies ran while one was open for 44% -> 11% of each run, Pallas kernels for 0% -> 17%
where the time goes in v1:
time: 1030 us; the launch traced here: 1020 us
  waiting for transfers between devices  562 us (55%)
  Pallas kernels  182 us (18%)
  starting transfers between devices  85.6 us (8%)
  blocking collectives  53.4 us (5%)
  matrix products  53.4 us (5%)
  local copies, waits for them, and re-layouts  46.3 us (4%)
  other arithmetic  20.3 us (2%)
  between operations  18.4 us (2%)
    all_gather x6, waiting for transfers between devices, gather_columns(): return lax.all_gather(shard, ALL, axis=1, tiled=True)  330 us
    unnamed x13, waiting for transfers between devices  191 us
    ppermute x14, starting transfers between devices, to_core(): return lax.ppermute(value, 'core', [(1 - core, core)])  61.8 us
    pallas_call x1, Pallas kernels, enc_backward(): pl.pallas_call(enc_backward_kernel, in_specs=whole(9), out_shape=[jax.Sha...  45.8 us
    pallas_call x1, Pallas kernels, enc_forward(): pl.pallas_call(enc_forward_kernel, in_specs=whole(7), out_shape=[jax.Shap...  43.6 us
    psum x1, blocking collectives, local(): lax.psum((jnp.sum(loss_rows[:, 0]), init_grad, gain_grad.reshape(-1), shi...  41.2 us
    pallas_call x1, Pallas kernels, attend_back(): pl.pallas_call(attend_back_kernel, in_specs=specs, out_shape=[jax.ShapeDt...  40.5 us
    pallas_call x1, Pallas kernels, attend(): pl.pallas_call(attend_kernel, in_specs=specs, out_shape=[grid] * 5 + [jax...  36.5 us
  transfers between devices with their start and end apart: 31, of which 15 were waited for; matrix products, arithmetic and copies ran while one was open for 11% of the time, Pallas kernels for 17%

profile of v1, /device:TPU:0, one launch (start us, length us, event | category | flops | bytes accessed | tf_op | source)
XLA Modules:
  0.0 1021.0 jit_solution(17785857340713413317)
XLA Ops:
  17.1 12.2 %all-gather = s32[4,4,32]{2,1,0:T(4,128)S(1)} all-gather(s32[1,4,32]{2,1,0:T(4,128)} %bitcast.163), channel_id=1, replica_groups=mesh['batch'=4,'chip'=4,'core'=2] {'batch'}, dimensions={0}, use_global_device_ids=true | all-gather | bytes 2560 | tf_op jit(solution)/shard_map/all_gather | solution.py:670
  53.0 29.3 %all-gather.14.cloned.1.call-done.in_ref = bf16[512,4096]{1,0:T(8,128)(2,1)} async-done(((bf16[512,128]{1,0:T(8,128)(2,1)}), bf16[512,4096]{1,0:T(8,128)(2,1)}) %all-gather.14.cloned.1.call-update) | async-done | bytes 4194320 | tf_op jit(solution)/shard_map/all_gather | solution.py:623
  82.3 93.3 %all-gather.16.cloned.1.call-done.weight_ref = bf16[1024,4096]{1,0:T(8,128)(2,1)} async-done(((bf16[1024,128]{1,0:T(8,128)(2,1)}), bf16[1024,4096]{1,0:T(8,128)(2,1)}) %all-gather.16.cloned.1.call-update) | async-done | bytes 8388624 | tf_op jit(solution)/shard_map/all_gather | solution.py:623
  175.7 43.6 %enc_forward.1 = (bf16[16,32,1024]{2,1,0:T(8,128)(2,1)}, f32[16,32,4096]{2,1,0:T(8,128)}, f32[16,32,1024]{2,1,0:T(8,128)}, f32[16,32,128]{2,1,0:T(8,128)}) custom-call(s32[1]{0:T(128)} %bitcast.core_ref, bf16[512,512]{1,0:T(8,128)(2,1)} %bitcast.127, bf16[512,4096]{1,0:T(8,128)(2,1)} %all-gather.14.cloned.1.call-done.in_ref, ...), custom_call_target="tpu_custom_call" | custom-call | tf_op jit(solution)/shard_map/enc_forward/pallas_call | solution.py:219
  229.1 39.9 %all-gather.10.cloned.1.call-done.weight_ref = bf16[1024,4096]{1,0:T(8,128)(2,1)} async-done(((bf16[1024,128]{1,0:T(8,128)(2,1)}), bf16[1024,4096]{1,0:T(8,128)(2,1)}) %all-gather.10.cloned.1.call-update) | async-done | bytes 8388624 | tf_op jit(solution)/shard_map/all_gather | solution.py:623
  280.4 51.4 %all-gather.20.cloned.1.call-done = bf16[2048,1024]{0,1:T(8,128)(2,1)} async-done(((bf16[2048,32]{0,1:T(8,128)(2,1)}), bf16[2048,1024]{0,1:T(8,128)(2,1)}) %all-gather.20.cloned.1.call-update) | async-done | bytes 4194320 | tf_op jit(solution)/shard_map/all_gather | solution.py:623
  331.9 6.4 copy.69.proj_ref
  338.3 57.0 %all-gather.12.cloned.1.call-done = bf16[1024,2048]{0,1:T(8,128)(2,1)} async-done(((bf16[1024,64]{0,1:T(8,128)(2,1)}), bf16[1024,2048]{0,1:T(8,128)(2,1)}) %all-gather.12.cloned.1.call-update) | async-done | bytes 4194320 | tf_op jit(solution)/shard_map/all_gather | solution.py:623
  399.6 59.0 %all-gather.18.cloned.1.call-done = bf16[1024,2048]{0,1:T(8,128)(2,1)} async-done(((bf16[1024,64]{0,1:T(8,128)(2,1)}), bf16[1024,2048]{0,1:T(8,128)(2,1)}) %all-gather.18.cloned.1.call-update) | async-done | bytes 4194320 | tf_op jit(solution)/shard_map/all_gather | solution.py:623
  458.6 6.5 fusion.29.key_ref
  465.1 36.5 %attend.1 = (f32[16,512]{1,0:T(8,128)}, f32[16,512]{1,0:T(8,128)}, f32[16,512]{1,0:T(8,128)}, f32[16,512]{1,0:T(8,128)}, f32[16,512]{1,0:T(8,128)}, /*index=5*/bf16[16,512]{1,0:T(8,128)(2,1)}, bf16[16,1024]{1,0:T(8,128)(2,1)}) custom-call(f32[2]{0:T(128)} %pad_maximum_fusion.5.scalar_ref, s32[1]{0:T(128)} %dynamic_slice.14.length_ref, ...), custom_call_target="tpu_custom_call" | custom-call | tf_op jit(solution)/shard_map/attend/pallas_call | solution.py:416
  501.6 15.3 %all-gather.22.cloned.1.call-done.out_w_ref = bf16[1024,1000]{1,0:T(8,128)(2,1)} async-done(((bf16[32,1000]{1,0:T(8,128)(2,1)}), bf16[1024,1000]{1,0:T(8,128)(2,1)}) %all-gather.22.cloned.1.call-update) | async-done | bytes 2048016 | tf_op jit(solution)/shard_map/all_gather | solution.py:717
  524.8 40.5 %attend_back.1 = (bf16[512,2048]{1,0:T(8,128)(2,1)}, f32[16,2048]{1,0:T(8,128)}, f32[2,1024]{1,0:T(2,128)}, f32[1,128]{1,0:T(1,128)}) custom-call(f32[2]{0:T(128)} %pad_maximum_fusion.5.scalar_ref, s32[1]{0:T(128)} %dynamic_slice.14.length_ref, bf16[16,1024]{1,0:T(8,128)(2,1)} %get-tuple-element.68.grad_ref, bf16[512,1024]{1,0:T(8,128)(2,1)} %copy-done.2, ...), custom_call_target="tpu_custom_call" | custom-call | tf_op jit(solution)/shard_map/attend_back/pallas_call | solution.py:526
  585.8 45.8 %enc_backward.1 = (bf16[16,32,4096]{2,1,0:T(8,128)(2,1)}, f32[1,4096]{1,0:T(1,128)}, f32[1,4096]{1,0:T(1,128)}, f32[2,1024]{1,0:T(2,128)}) custom-call(s32[1]{0:T(128)} %bitcast.core_ref, f32[16,32,4096]{2,1,0:T(8,128)} %get-tuple-element.64.norm_ref, f32[16,32,1024]{2,1,0:T(8,128)} %get-tuple-element.65.cell_ref, ...), custom_call_target="tpu_custom_call" | custom-call | tf_op jit(solution)/shard_map/enc_backward/pallas_call | solution.py:312
  631.7 7.7 bitcast_convert_fusion.1
  639.3 6.5 copy.78
  647.2 9.1 bitcast_convert_fusion
  656.2 12.0 %copy.80 = bf16[1024,4096]{0,1:T(8,128)(2,1)} copy(bf16[1024,4096]{1,0:T(8,128)(2,1)} %bitcast_convert_fusion) | data formatting | bytes 16777216
  692.9 7.7 all-to-all-done.4
  709.0 42.0 %collective-permute-start.5 = (bf16[8,32,512]{2,1,0:T(8,128)(2,1)S(1)}, bf16[8,32,512]{2,1,0:T(8,128)(2,1)}, u32[]{:S(2)}, u32[]{:S(2)}) collective-permute-start(bf16[8,32,512]{2,1,0:T(8,128)(2,1)S(1)} %slice_bitcast_fusion), channel_id=1, source_target_pairs={{0,1},{2,3},{4,5},{6,7},{8,9},{10,11},{12,13},{14,15},{16,17},{18,... | collective-permute-start | bytes 786440 | tf_op jit(solution)/shard_map/ppermute | solution.py:619
  753.1 41.2 %all-reduce.2 = (f32[]{:T(128)}, f32[4096]{0:T(1024)}, f32[4096]{0:T(1024)}, f32[2,1024]{1,0:T(2,128)}, f32[2,1024]{1,0:T(2,128)}, /*index=5*/f32[2,1024]{1,0:T(...) all-reduce(f32[]{:T(128)} %slice_reduce_fusion, ...), channel_id=1, replica_groups=mesh['batch'=4,'chip'=4,'core'=2] {'batch','chip','core'}, use_global_device_ids=true, to_apply=%region_2.3 | all-reduce | flops 16363 | bytes 130904 | tf_op jit(solution)/shard_map/psum | solution.py:839
  800.0 8.0 all-to-all-done.3
  824.1 41.0 %reduce-scatter.10.cloned.1.call-done = bf16[128,512]{1,0:T(8,128)(2,1)} async-done(((bf16[4096,512]{1,0:T(8,128)(2,1)}), bf16[128,512]{1,0:T(8,128)(2,1)}) %reduce-scatter.10.cloned.1.call-update) | async-done | bytes 131088
  866.9 145.1 %reduce-scatter.12.cloned.1.call-done = bf16[128,1024]{1,0:T(8,128)(2,1)} async-done(((bf16[4096,1024]{1,0:T(8,128)(2,1)}), bf16[128,1024]{1,0:T(8,128)(2,1)}) %reduce-scatter.12.cloned.1.call-update) | async-done | bytes 262160
  (206 shorter events, 145.6 us)
Async XLA Ops:
  7.2 75.1 %all-gather.14.cloned.1.call-start = ((), (), s32[]{:S(2)}) async-start(), calls=%async_computation.10 | async-start | bytes 4325376 | tf_op jit(solution)/shard_map/all_gather | solution.py:623
  7.9 167.7 %all-gather.16.cloned.1.call-start = ((), (), s32[]{:S(2)}) async-start(), calls=%async_computation.11 | async-start | bytes 8650752 | tf_op jit(solution)/shard_map/all_gather | solution.py:623
  8.7 260.3 %all-gather.10.cloned.1.call-start = ((), (), s32[]{:S(2)}) async-start(), calls=%async_computation.8 | async-start | bytes 8650752 | tf_op jit(solution)/shard_map/all_gather | solution.py:623
  9.4 322.4 %all-gather.20.cloned.1.call-start = ((), (), s32[]{:S(2)}) async-start(), calls=%async_computation.13 | async-start | bytes 4325376 | tf_op jit(solution)/shard_map/all_gather | solution.py:623
  10.0 385.3 %all-gather.12.cloned.1.call-start = ((), (), s32[]{:S(2)}) async-start(), calls=%async_computation.9 | async-start | bytes 4325376 | tf_op jit(solution)/shard_map/all_gather | solution.py:623
  10.6 448.0 %all-gather.18.cloned.1.call-start = ((), (), s32[]{:S(2)}) async-start(), calls=%async_computation.12 | async-start | bytes 4325376 | tf_op jit(solution)/shard_map/all_gather | solution.py:623
  11.2 505.7 %all-gather.22.cloned.1.call-start = ((), (), s32[]{:S(2)}) async-start(), calls=%async_computation.14 | async-start | bytes 2162688 | tf_op jit(solution)/shard_map/all_gather | solution.py:717
  11.9 17.6 %all-to-all-start.1 = ((bf16[8,32,512]{2,1,0:T(8,128)(2,1)}), bf16[8,32,512]{2,1,0:T(8,128)(2,1)S(1)}, u32[]{:S(2)}, u32[]{:S(2)}) async-start(bf16[8,32,512]{2,1,0:T(8,128)(2,1)} %bitcast.142), calls=%async_computation.1 | async-start | bytes 524288 | tf_op jit(solution)/shard_map/all_to_all | solution.py:690
  29.5 22.4 %collective-permute-start.2 = (bf16[8,32,512]{2,1,0:T(8,128)(2,1)S(1)}, bf16[8,32,512]{2,1,0:T(8,128)(2,1)S(1)}, u32[]{:S(2)}, u32[]{:S(2)}) collective-permute-start(bf16[8,32,512]{2,1,0:T(8,128)(2,1)S(1)} %all-to-all-done.1), channel_id=1, source_target_pairs={{1,0},{3,2},{5,4},{7,6},{9,8},{11,10},{13,12},{15,14},{17,16},{19,... | collective-permute-start | bytes 786440 | tf_op jit(solution)/shard_map/ppermute | solution.py:619
  32.0 16.2 %all-to-all-start = ((bf16[16,32,128]{2,1,0:T(8,128)(2,1)}), bf16[16,32,128]{2,1,0:T(8,128)(2,1)S(1)}, u32[]{:S(2)}, u32[]{:S(2)}) async-start(bf16[16,32,128]{2,1,0:T(8,128)(2,1)} %bitcast.3), calls=%async_computation | async-start | bytes 262144 | tf_op jit(solution)/shard_map/all_to_all | solution.py:677
  48.1 230.2 %all-to-all-start.2 = ((f32[8,1,1024]{2,1,0:T(1,128)}), f32[8,1,1024]{2,1,0:T(1,128)S(1)}, u32[]{:S(2)}, u32[]{:S(2)}) async-start(f32[8,1,1024]{2,1,0:T(1,128)} %reshape.200), calls=%async_computation.2 | async-start | bytes 65536 | tf_op jit(solution)/shard_map/all_to_all | solution.py:700
  51.5 757.3 %all-gather.24.cloned.1.call-start = ((), (), s32[]{:S(2)}) async-start(), calls=%async_computation.15 | async-start | bytes 3244032 | tf_op jit(solution)/shard_map/all_gather | solution.py:799
  51.5 175.8 %collective-permute-start = (bf16[16,32,128]{2,1,0:T(8,128)(2,1)S(1)}, bf16[16,32,128]{2,1,0:T(8,128)(2,1)S(1)}, u32[]{:S(2)}, u32[]{:S(2)}) collective-permute-start(bf16[16,32,128]{2,1,0:T(8,128)(2,1)S(1)} %all-to-all-done), channel_id=1, source_target_pairs={{0,1},{1,0},{2,3},{3,2},{4,5},{5,4},{6,7},{7,6},{8,9},{9,8},{10,11... | collective-permute-start | bytes 393224 | tf_op jit(solution)/shard_map/ppermute | solution.py:615
  221.1 178.3 %collective-permute-start.3 = (bf16[512,1024]{1,0:T(8,128)(2,1)S(1)}, bf16[512,1024]{1,0:T(8,128)(2,1)}, u32[]{:S(2)}, u32[]{:S(2)}) collective-permute-start(bf16[512,1024]{1,0:T(8,128)(2,1)S(1)} %bitcast.125), channel_id=1, source_target_pairs={{0,1},{2,3},{4,5},{6,7},{8,9},{10,11},{12,13},{14,15},{16,17},{18,... | collective-permute-start | bytes 3145736 | tf_op jit(solution)/shard_map/ppermute | solution.py:619
  274.4 63.8 %collective-permute-start.1 = (bf16[32,1024]{1,0:T(8,128)(2,1)S(1)}, bf16[32,1024]{1,0:T(8,128)(2,1)S(1)}, u32[]{:S(2)}, u32[]{:S(2)}) collective-permute-start(bf16[32,1024]{1,0:T(8,128)(2,1)S(1)} %convert_element_type.71), channel_id=1, source_target_pairs={{1,0},{3,2},{5,4},{7,6},{9,8},{11,10},{13,12},{15,14},{17,16},{19,... | collective-permute-start | bytes 196616 | tf_op jit(solution)/shard_map/ppermute | solution.py:619
  524.8 297.7 %reduce-scatter.8.cloned.1.call-start = ((), (), s32[]{:S(2)}) async-start(), calls=%async_computation.16 | async-start | bytes 4325376 | tf_op jit(solution)/shard_map/reduce_scatter | solution.py:782
  571.7 293.5 %reduce-scatter.10.cloned.1.call-start = ((), (), s32[]{:S(2)}) async-start(), calls=%async_computation.17 | async-start | bytes 4325376
  645.8 366.2 %reduce-scatter.12.cloned.1.call-start = ((), (), s32[]{:S(2)}) async-start(), calls=%async_computation.18 | async-start | bytes 8650752
  668.9 10.1 collective-permute-start.7
  671.6 14.4 %collective-permute-start.6 = (bf16[16,2048]{1,0:T(8,128)(2,1)S(1)}, bf16[16,2048]{1,0:T(8,128)(2,1)S(1)}, u32[]{:S(2)}, u32[]{:S(2)}) collective-permute-start(bf16[16,2048]{1,0:T(8,128)(2,1)S(1)} %get-tuple-element.101), channel_id=1, source_target_pairs={{1,0},{3,2},{5,4},{7,6},{9,8},{11,10},{13,12},{15,14},{17,16},{19,... | collective-permute-start | bytes 196616 | tf_op jit(solution)/shard_map/ppermute | solution.py:619
  686.9 13.7 %all-to-all-start.4 = ((bf16[16,32,256]{2,1,0:T(8,128)(2,1)}), bf16[16,32,256]{2,1,0:T(8,128)(2,1)S(1)}, u32[]{:S(2)}, u32[]{:S(2)}) async-start(bf16[16,32,256]{2,1,0:T(8,128)(2,1)} %fusion.14), calls=%async_computation.4 | async-start | bytes 524288 | tf_op jit(solution)/shard_map/all_to_all | solution.py:817
  701.5 97.7 %collective-permute-start.10 = (f32[1000,128]{1,0:T(8,128)S(1)}, f32[1000,128]{1,0:T(8,128)S(1)}, u32[]{:S(2)}, u32[]{:S(2)}) collective-permute-start(f32[1000,128]{1,0:T(8,128)S(1)} %split.40), channel_id=1, source_target_pairs={{1,0},{3,2},{5,4},{7,6},{9,8},{11,10},{13,12},{15,14},{17,16},{19,... | collective-permute-start | bytes 1536008 | tf_op jit(solution)/shard_map/ppermute | solution.py:619
  709.0 85.2 %collective-permute-start.5 = (bf16[8,32,512]{2,1,0:T(8,128)(2,1)S(1)}, bf16[8,32,512]{2,1,0:T(8,128)(2,1)}, u32[]{:S(2)}, u32[]{:S(2)}) collective-permute-start(bf16[8,32,512]{2,1,0:T(8,128)(2,1)S(1)} %slice_bitcast_fusion), channel_id=1, source_target_pairs={{0,1},{2,3},{4,5},{6,7},{8,9},{10,11},{12,13},{14,15},{16,17},{18,... | collective-permute-start | bytes 786440 | tf_op jit(solution)/shard_map/ppermute | solution.py:619
  795.0 13.0 %all-to-all-start.3 = ((bf16[8,32,512]{2,1,0:T(8,128)(2,1)}), bf16[8,32,512]{2,1,0:T(8,128)(2,1)S(1)}, u32[]{:S(2)}, u32[]{:S(2)}) async-start(bf16[8,32,512]{2,1,0:T(8,128)(2,1)} %fusion.15), calls=%async_computation.3 | async-start | bytes 524288 | tf_op jit(solution)/shard_map/all_to_all | solution.py:789
  (37 other events, 1135.3 us)
Sparse Core Ops, SparseCore 0:
  10.9 71.3 all-gather.13
  85.2 90.4 all-gather.15
  178.5 90.4 all-gather.9
  271.7 60.0 all-gather.19
  334.6 60.6 all-gather.11
  398.0 60.5 all-gather.17
  461.5 55.3 all-gather.21
  524.9 57.7 all-gather.23
  585.0 140.0 reduce-scatter.7
  727.3 137.8 reduce-scatter.9
  867.5 144.5 reduce-scatter.11
